TPU v7x, 512 devices: a whole 4x8x8 slice. The times are simulated.
512 devices in a mesh: ctx: 32 (over z, x_lo, core), head: 16 (over x_hi, y).
Axes of the slice: x: 4 (x_hi: 2, x_lo: 2; x = x_hi * 2 + x_lo), y: 8, z: 8, core: 2. Of those that a mesh axis runs over, the one named last changes fastest.
Arguments:
- q_latent: bfloat16 [4096, 1536], P('ctx', 'head'), may hold values from -72 to 72
- latent_cache: bfloat16 [4096, 576], P('ctx'), may hold values from -6 to 6
- w_q_up: bfloat16 [1536, 12288], P(None, 'head'), may hold values from -0.15625 to 0.15625
- w_kv_up: bfloat16 [512, 16384], P(None, 'head'), may hold values from -0.25 to 0.25
- w_out: bfloat16 [8192, 7168], P('head', 'ctx'), may hold values from -0.5 to 0.5
- token_pos: int32 [4096], P('ctx'), may hold values from 0 to 4095, as said below
- start_offset: int32 [1], replicated, may hold values from 0 to 65535
Outputs:
- layer_out: bfloat16 [4096, 7168], P('ctx', 'head')
Inputs may be any that keep to these rules, and one draw needn't show every extreme that they name: `token_pos`: a permutation of 0 to 4095; the 128 tokens of each index of ctx hold consecutive positions in increasing order.
All inputs are finite; a program needn't handle non-finite values.
Results may differ from a plain program's by a relative error of at most 0.035.
Values may be sent and summed in bfloat16 or wider, within the bound.
No kernel may reach another device: no remote copies, remote signals or barrier semaphores. Data moves between devices by JAX's collectives and lax.ppermute only.
A program may use at most 64 MiB of HBM per device.

v0:
```python
import jax
import jax.numpy as jnp
from jax import lax
from jax.sharding import PartitionSpec as P

KVL = 512
NOPE = 128
ROPE = 64
VDIM = 128


negative_fill = -1e30
softmax_scale = 0.135
rope_base = 10000.0


def sent_to_all(array, axis):
    copies = jnp.broadcast_to(array, (lax.axis_size(axis), *array.shape))
    return lax.all_to_all(copies, axis, split_axis=0, concat_axis=0, tiled=True)


def in_order(tiles, dim):
    tiles = jnp.moveaxis(tiles, 0, dim)
    dims = tiles.shape
    return tiles.reshape(*dims[:dim], dims[dim] * dims[dim + 1], *dims[dim + 2 :])


def gathered_copies(array, axis, dim):
    tiles = sent_to_all(array, axis)
    return in_order(tiles, dim)


def split_up(array, dim, devices):
    before, after = (array.shape[:dim], array.shape[dim + 1 :])
    return jnp.moveaxis(array.reshape(*before, devices, -1, *after), dim, 0)


def summed_on_arrival(array, axis, dim):
    tiles = split_up(array, dim, lax.axis_size(axis))
    arrived = lax.all_to_all(tiles, axis, split_axis=0, concat_axis=0, tiled=True)
    return arrived.astype(jnp.float32).sum(axis=0)


def rotate(values, angle):
    half = ROPE // 2
    cosine = jnp.cos(angle)
    sine = jnp.sin(angle)
    first = values[..., :half]
    second = values[..., half:]
    return jnp.concatenate(
        [first * cosine - second * sine, first * sine + second * cosine], axis=-1
    )


def shards(q_latent, latent_cache, w_q_up, w_kv_up, w_out, token_pos, start_offset):
    features = gathered_copies(q_latent, "head", 1)
    row_count = features.shape[0]
    head_count = w_q_up.shape[1] // (NOPE + ROPE)
    query = jnp.dot(features, w_q_up, preferred_element_type=jnp.float32).reshape(
        row_count, head_count, NOPE + ROPE
    )
    absolute = (token_pos + start_offset[0]).astype(jnp.float32)
    freqs = rope_base ** (-jnp.arange(ROPE // 2, dtype=jnp.float32) * 2.0 / ROPE)
    angle = absolute[:, None, None] * freqs[None, None, :]
    query_nope = query[..., :NOPE].astype(jnp.bfloat16)
    query_rope = rotate(query[..., NOPE:], angle).astype(jnp.bfloat16)
    kv_weights = w_kv_up.reshape(KVL, head_count, NOPE + VDIM)
    query_main = jnp.einsum(
        "rhn,chn->rhc", query_nope, kv_weights[:, :, :NOPE], preferred_element_type=jnp.float32
    ).astype(jnp.bfloat16)
    value_width = KVL

    def attend(carry, block, key_pos):
        maxima, totals, accum = carry
        latent = block[:, :KVL]
        key_rope = block[:, KVL:]
        scores = jnp.einsum("rhd,kd->hrk", query_rope, key_rope, preferred_element_type=jnp.float32)
        scores = scores + jnp.einsum(
            "rhc,kc->hrk", query_main, latent, preferred_element_type=jnp.float32
        )
        visible = key_pos[None, None, :] <= token_pos[None, :, None]
        scores = jnp.where(visible, scores * softmax_scale, negative_fill)
        new_max = jnp.maximum(maxima, jnp.max(scores, axis=-1))
        weights = jnp.where(visible, jnp.exp(scores - new_max[..., None]), 0.0)
        factor = jnp.exp(maxima - new_max)
        totals = totals * factor + jnp.sum(weights, axis=-1)
        rounded = weights.astype(jnp.bfloat16)
        addition = jnp.einsum("hrk,kc->hrc", rounded, latent, preferred_element_type=jnp.float32)
        return (new_max, totals, accum * factor[..., None] + addition)

    def visit(carry, block, key_pos):
        return attend(carry, block, key_pos)

    initial = (
        jnp.full((head_count, row_count), negative_fill, jnp.float32),
        jnp.zeros((head_count, row_count), jnp.float32),
        jnp.zeros((head_count, row_count, value_width), jnp.float32),
    )
    carry = initial
    block = lax.all_gather(latent_cache, "ctx", axis=0, tiled=True)
    key_pos = lax.all_gather(token_pos, "ctx", axis=0, tiled=True)
    length = block.shape[0]
    count = length // 512

    def scan_step(state, inputs):
        return (visit(state, inputs[0], inputs[1]), None)

    carry, unused = lax.scan(
        scan_step, carry, (block.reshape(count, 512, block.shape[1]), key_pos.reshape(count, 512))
    )
    maxima, totals, accum = carry
    normed = accum / totals[..., None]
    heads_out = jnp.einsum(
        "hrc,chv->rhv",
        normed.astype(jnp.bfloat16),
        kv_weights[:, :, NOPE:],
        preferred_element_type=jnp.float32,
    ).astype(jnp.bfloat16)
    attention = heads_out.reshape(row_count, head_count * VDIM)
    partial_value = jnp.dot(
        attention,
        lax.all_gather(w_out, "ctx", axis=1, tiled=True),
        preferred_element_type=jnp.float32,
    )
    summed = summed_on_arrival(partial_value.astype(jnp.bfloat16), "head", 1)
    return summed.astype(jnp.bfloat16)


def solution(mesh):
    in_specs = (
        P("ctx", "head"),
        P("ctx", None),
        P(None, "head"),
        P(None, "head"),
        P("head", "ctx"),
        P("ctx"),
        P(),
    )
    out_specs = P("ctx", "head")
    return jax.shard_map(shards, mesh=mesh, in_specs=in_specs, out_specs=out_specs, check_vma=False)
```

profile of v0, /device:TPU:1, one launch (start us, length us, event | category | flops | bytes accessed | tf_op | source)
XLA Modules:
  0.0 238.1 jit_solution(306329421979309599)
XLA Ops:
  6.5 0.7 all-gather.4.cloned.1.call-update
  7.3 1.6 broadcast_in_dim.40
  8.8 10.3 %all-to-all-start = ((bf16[16,128,96]{1,2,0:T(8,128)(2,1)}), bf16[16,128,96]{1,2,0:T(8,128)(2,1)}, u32[]{:S(2)}, u32[]{:S(2)}) async-start(bf16[16,128,96]{1,2,0:T(8,128)(2,1)} %broadcast_in_dim.40), calls=%async_computation | async-start | bytes 786432 | tf_op jit(solution)/shard_map/all_to_all | solution.py:19
  19.1 0.7 all-gather.6.cloned.1.call-update
  19.9 2.8 %copy.28 = bf16[1536,768]{0,1:T(8,128)(2,1)S(1)} copy(bf16[1536,768]{1,0:T(8,128)(2,1)} %param.11) | data formatting | bytes 4718592 | tf_op args[2]
  23.4 2.3 copy.30
  25.6 39.9 %all-gather = s32[32,1,128]{2,1,0:T(1,128)S(1)} all-gather(s32[1,1,128]{2,1,0:T(1,128)S(1)} %bitcast.69), channel_id=1, replica_groups=mesh['ctx'=32,'head'=16] {'ctx'}, dimensions={0}, use_global_device_ids=true | all-gather | bytes 16896 | tf_op jit(solution)/shard_map/all_gather | solution.py:101
  65.6 0.5 broadcast.97
  66.1 0.6 reduce.4
  66.8 0.1 multiply_cosine_fusion
  66.9 1.9 fusion.16
  68.8 0.3 fusion.12
  69.2 23.3 %all-gather.4.cloned.1.call-done = bf16[4096,576]{0,1:T(8,128)(2,1)} async-done(((bf16[128,576]{0,1:T(8,128)(2,1)}), bf16[4096,576]{0,1:T(8,128)(2,1)}) %all-gather.4.cloned.1.call-update) | async-done | bytes 4718608 | tf_op jit(solution)/shard_map/all_gather | solution.py:100
  92.5 4.9 %copy.46 = bf16[72,8,8,512]{3,2,0,1:T(8,128)(2,1)} copy(bf16[72,8,8,512]{3,2,1,0:T(8,128)(2,1)} %bitcast.64) | data formatting | bytes 9437184 | tf_op jit(solution)/shard_map/reshape | solution.py:109
  97.4 23.6 %while.15 = (s32[]{:T(128)}, f32[4,128]{1,0:T(4,128)S(1)}, f32[4,128]{1,0:T(4,128)S(1)}, f32[4,128,512]{2,1,0:T(8,128)S(1)}, s32[8,512]{1,0:T(8,128)S(1)}, /*ind...) while((s32[]{:T(128)}, f32[4,128]{1,0:T(4,128)S(1)}, ...), condition=%wide.region_3.4_spmd.clone, body=%wide.region_0.3_spmd.clone.sunk | while | flops 573901312 | bytes 10525313 | solution.py:108
  97.4 1.1 dynamic-slice_bitcast_fusion.2
  98.5 0.3 fusion.33
  98.9 0.1 broadcast_compare_fusion.2
  99.0 0.5 fusion.34
  99.5 0.2 fusion.35
  99.8 0.6 convolution_add_fusion.3
  100.4 1.1 dynamic-slice_bitcast_fusion.2
  101.5 0.3 fusion.33
  101.8 0.1 broadcast_compare_fusion.2
  102.0 0.5 fusion.34
  102.5 0.2 fusion.35
  102.7 0.6 convolution_add_fusion.3
  103.3 1.1 dynamic-slice_bitcast_fusion.2
  104.4 0.3 fusion.33
  104.8 0.1 broadcast_compare_fusion.2
  104.9 0.5 fusion.34
  105.5 0.2 fusion.35
  105.7 0.6 convolution_add_fusion.3
  106.3 1.1 dynamic-slice_bitcast_fusion.2
  107.4 0.3 fusion.33
  107.9 0.5 fusion.34
  108.4 0.2 fusion.35
  108.6 0.6 convolution_add_fusion.3
  109.2 1.1 dynamic-slice_bitcast_fusion.2
  110.4 0.3 fusion.33
  110.8 0.5 fusion.34
  111.4 0.2 fusion.35
  111.6 0.6 convolution_add_fusion.3
  112.2 1.1 dynamic-slice_bitcast_fusion.2
  113.3 0.3 fusion.33
  113.8 0.5 fusion.34
  114.3 0.2 fusion.35
  114.6 0.6 convolution_add_fusion.3
  115.2 1.1 dynamic-slice_bitcast_fusion.2
  116.3 0.3 fusion.33
  116.7 0.5 fusion.34
  117.3 0.2 fusion.35
  117.5 0.6 convolution_add_fusion.3
  118.1 1.1 dynamic-slice_bitcast_fusion.2
  119.2 0.3 fusion.33
  119.7 0.5 fusion.34
  120.3 0.2 fusion.35
  120.5 0.6 convolution_add_fusion.3
  121.1 1.4 convolution_convert_fusion.2
  122.5 46.4 %all-gather.6.cloned.1.call-done = bf16[512,7168]{0,1:T(8,128)(2,1)} async-done(((bf16[512,224]{0,1:T(8,128)(2,1)}), bf16[512,7168]{0,1:T(8,128)(2,1)}) %all-gather.6.cloned.1.call-update) | async-done | bytes 7340048 | tf_op jit(solution)/shard_map/all_gather | solution.py:122
  168.9 5.6 %convolution_convert_fusion = bf16[128,7168]{1,0:T(8,128)(2,1)S(1)} fusion(bf16[128,512]{0,1:T(8,128)(2,1)S(1)} %bitcast.67, bf16[512,7168]{0,1:T(8,128)(2,1)} %all-gather.6.cloned.1.call-done), kind=kOutput, calls=%fused_computation.23 | convolution fusion | flops 940441600 | bytes 9306112 | tf_op jit(solution)/shard_map/dot_general | solution.py:120
  174.5 2.3 copy.34
  176.8 53.5 %all_to_all.10 = bf16[16,128,448]{1,2,0:T(8,128)(2,1)S(1)} all-to-all(bf16[16,128,448]{1,2,0:T(8,128)(2,1)} %bitcast.63), channel_id=1, replica_groups=mesh['ctx'=32,'head'=16] {'head'}, dimensions={0} | all-to-all | bytes 3670016 | tf_op jit(solution)/shard_map/all_to_all | solution.py:40
  230.3 0.9 reduce_sum.21
  (52 shorter events, 1.1 us)
Async XLA Ops:
  6.5 86.0 %all-gather.4.cloned.1.call-start = ((), (), s32[]{:S(2)}) async-start(), calls=%async_computation.2 | async-start | bytes 4866048 | tf_op jit(solution)/shard_map/all_gather | solution.py:100
  8.8 58.1 %all-to-all-start = ((bf16[16,128,96]{1,2,0:T(8,128)(2,1)}), bf16[16,128,96]{1,2,0:T(8,128)(2,1)}, u32[]{:S(2)}, u32[]{:S(2)}) async-start(bf16[16,128,96]{1,2,0:T(8,128)(2,1)} %broadcast_in_dim.40), calls=%async_computation | async-start | bytes 786432 | tf_op jit(solution)/shard_map/all_to_all | solution.py:19
  19.1 149.8 %all-gather.6.cloned.1.call-start = ((), (), s32[]{:S(2)}) async-start(), calls=%async_computation.3 | async-start | bytes 7569408 | tf_op jit(solution)/shard_map/all_gather | solution.py:122
  19.9 5.8 %copy-start.1 = (s32[128]{0:T(128)S(1)}, s32[128]{0:T(128)}, u32[]{:S(2)}) copy-start(s32[128]{0:T(128)} %param.14) | copy-start | bytes 1540
  66.9 1.9 copy-start
Sparse Core Ops, SparseCore 0:
  9.4 83.0 all-gather.3
  94.7 74.1 all-gather.5
where the time goes:
time: 240 us; the launch traced here: 238 us
  blocking collectives  93.5 us (39%)
  waiting for transfers between devices  71.1 us (30%)
  local copies, waits for them, and re-layouts  23.4 us (10%)
  matrix products  20.4 us (8%)
  between operations  14.2 us (6%)
  starting transfers between devices  10.3 us (4%)
  other arithmetic  4.64 us (2%)
    all_to_all x1, blocking collectives, summed_on_arrival(): lax.all_to_all(tiles, axis, split_axis=0, concat_axis=0, tiled=True)  53.5 us
    all_gather x1, waiting for transfers between devices, shards(): lax.all_gather(w_out, 'ctx', axis=1, tiled=True)  46.4 us
    all_gather x1, blocking collectives, shards(): key_pos = lax.all_gather(token_pos, 'ctx', axis=0, tiled=True)  39.9 us
    all_gather x1, waiting for transfers between devices, shards(): block = lax.all_gather(latent_cache, 'ctx', axis=0, tiled=True)  23.3 us
    all_to_all x1, starting transfers between devices, sent_to_all(): return lax.all_to_all(copies, axis, split_axis=0, concat_axis=0, tiled=True)  10.3 us
    squeeze x8, local copies, waits for them, and re-layouts, shards(): lax.scan(scan_step, carry, (block.reshape(count, 512, block.shape[1]), ke...  8.87 us
    dot_general x1, matrix products, shards(): jnp.dot(attention, lax.all_gather(w_out, 'ctx', axis=1, tiled=True), pref...  5.58 us
    unnamed x6, local copies, waits for them, and re-layouts  5.12 us
  transfers between devices with their start and end apart: 3, of which 2 were waited for; matrix products, arithmetic and copies ran while one was open for 17% of the time, Pallas kernels for 0%

commit v1 on v0

v1 whole, which is shorter than its diff:
```python
import jax
import jax.numpy as jnp
from jax import lax
from jax.experimental import pallas as pl
from jax.experimental.pallas import tpu as pltpu
from jax.sharding import Mesh, PartitionSpec as P

QL = 1536
KVL = 512
NOPE = 128
ROPE = 64
VDIM = 128
HEADS = 4
TOK = 128
QD = NOPE + ROPE
KROWS = KVL + ROPE + 16
QROWS = HEADS * QD + 16
OROWS = HEADS * VDIM + 16

softmax_scale = 0.135
rope_base = 10000.0
masked = -1e30
floor = -1e29

F32 = jnp.float32
BF16 = jnp.bfloat16
CTX = ("z", "xl", "core")
NEAR = ("xl", "core")
VMEM = pl.BlockSpec(memory_space=pltpu.VMEM)
LIMIT = 56 * 1024 * 1024


def dot(a, b):
    return jnp.dot(a, b, preferred_element_type=F32)


def kernel_call(body, shape, args, scratch=(), flops=0):
    return pl.pallas_call(
        body,
        out_shape=jax.ShapeDtypeStruct(shape, BF16),
        in_specs=[VMEM] * len(args),
        out_specs=VMEM,
        scratch_shapes=list(scratch),
        compiler_params=pltpu.CompilerParams(vmem_limit_bytes=LIMIT),
        cost_estimate=pl.CostEstimate(flops=flops, bytes_accessed=4_000_000, transcendentals=0),
    )(*args)


def query_body(latent, weights, cosine, sine, pos, out):
    query = dot(weights[...], latent[...])
    cos, sin = cosine[...], sine[...]
    half = ROPE // 2
    for h in range(HEADS):
        base = h * QD
        out[base : base + NOPE, :] = query[base : base + NOPE].astype(BF16)
        a = query[base + NOPE : base + NOPE + half]
        b = query[base + NOPE + half : base + QD]
        out[base + NOPE : base + QD, :] = jnp.concatenate(
            [a * cos - b * sin, a * sin + b * cos], axis=0
        ).astype(BF16)
    out[HEADS * QD :, :] = pos[...]


def attend_body(queries, keys, w_key, w_value_t, out, latent, rope_keys, key_pos, key_cat, value_t):
    blocks = keys.shape[0]
    tokens = queries.shape[0]
    for z in range(blocks):
        rows = slice(z * TOK, (z + 1) * TOK)
        latent[rows, :] = keys[z, :KVL, :].T
        tail = keys[z, KVL:, :].astype(F32).T
        rope_keys[rows, :] = tail[:, :ROPE].astype(BF16)
        key_pos[rows, :] = tail[:, ROPE : ROPE + 1] * 64.0 + tail[:, ROPE + 1 : ROPE + 2]
        value_t[:, rows] = dot(w_value_t[...], keys[z, :KVL, :]).astype(BF16)
    expanded = dot(latent[...], w_key[...]).astype(BF16)
    for h in range(HEADS):
        key_cat[h, :, :NOPE] = expanded[:, h * NOPE : (h + 1) * NOPE]
        key_cat[h, :, NOPE:] = rope_keys[...]
    positions = key_pos[...]
    for pair in range(tokens // 2):
        two = (2 * pair, 2 * pair + 1)
        q_pos = jnp.concatenate(
            [queries[t, HEADS * QD : HEADS * QD + 2, :].astype(F32) for t in two], axis=1
        )
        q_pos = q_pos[0:1] * 64.0 + q_pos[1:2]
        visible = positions <= q_pos
        stats = []
        for h in range(HEADS):
            q = jnp.concatenate([queries[t, h * QD : (h + 1) * QD, :] for t in two], axis=1)
            scores = jnp.where(visible, dot(key_cat[h], q) * softmax_scale, masked)
            largest = jnp.maximum(jnp.max(scores, axis=0, keepdims=True), floor)
            weights = jnp.exp(scores - largest)
            total = jnp.sum(weights, axis=0, keepdims=True)
            some = total > 0.0
            safe = jnp.where(some, total, 1.0)
            summed = dot(value_t[h * VDIM : (h + 1) * VDIM, :], weights.astype(BF16)) / safe
            level = jnp.where(some, largest + jnp.log(safe), masked)
            first = level.astype(BF16)
            rest = level - first.astype(F32)
            second = rest.astype(BF16)
            third = (rest - second.astype(F32)).astype(BF16)
            stats += [first.astype(F32), second.astype(F32), third.astype(F32)]
            summed = summed.astype(BF16)
            for i, t in enumerate(two):
                out[t, h * VDIM : (h + 1) * VDIM, :] = summed[:, i * TOK : (i + 1) * TOK]
        stats = jnp.concatenate(stats + [jnp.zeros_like(stats[0])] * 4, axis=0).astype(BF16)
        for i, t in enumerate(two):
            out[t, HEADS * VDIM :, :] = stats[:, i * TOK : (i + 1) * TOK]


def merge_body(parts, out):
    count = parts.shape[0]
    tails = [parts[s, HEADS * VDIM :, :].astype(F32) for s in range(count)]
    for h in range(HEADS):
        levels = [t[3 * h : 3 * h + 1] + t[3 * h + 1 : 3 * h + 2] + t[3 * h + 2 : 3 * h + 3] for t in tails]
        top = levels[0]
        for level in levels[1:]:
            top = jnp.maximum(top, level)
        shares = [jnp.exp(level - top) for level in levels]
        rows = slice(h * VDIM, (h + 1) * VDIM)
        whole = sum(shares)
        added = sum(parts[s, rows, :].astype(F32) * shares[s] for s in range(count))
        out[rows, :] = (added / whole).astype(BF16)


def project_body(w, x, out):
    out[...] = (dot(w[0], x[0]) + dot(w[1], x[1])).astype(BF16)


def project(w, x, tiles):
    rows = w.shape[1] // tiles
    return pl.pallas_call(
        project_body,
        grid=(tiles,),
        out_shape=jax.ShapeDtypeStruct((w.shape[1], TOK), BF16),
        in_specs=[
            pl.BlockSpec((2, rows, w.shape[2]), lambda i: (0, i, 0)),
            pl.BlockSpec((2, x.shape[1], TOK), lambda i: (0, 0, 0)),
        ],
        out_specs=pl.BlockSpec((rows, TOK), lambda i: (i, 0)),
        compiler_params=pltpu.CompilerParams(vmem_limit_bytes=LIMIT),
        cost_estimate=pl.CostEstimate(
            flops=4 * w.shape[1] * w.shape[2] * TOK, bytes_accessed=8_000_000, transcendentals=0
        ),
    )(w, x)


def sent_to_all(array, axis):
    copies = jnp.broadcast_to(array, (lax.axis_size(axis), *array.shape))
    return lax.all_to_all(copies, axis, split_axis=0, concat_axis=0, tiled=True)


def crossed():
    pairs = []
    for z in range(8):
        for xh in range(2):
            source = z * 2 + xh
            target = source if z // 4 == xh else (z ^ 4) * 2 + (1 - xh)
            pairs.append((source, target))
    return pairs


def shards(q_latent, latent_cache, w_q_up, w_kv_up, w_out, token_pos, start_offset):
    pos_rows = jnp.concatenate(
        [(token_pos >> 6)[None], (token_pos & 63)[None], jnp.zeros((14, TOK), jnp.int32)], axis=0
    ).astype(BF16)

    w_mine = lax.ppermute(w_out.T, ("z", "xh"), crossed())
    w_all = lax.all_gather(w_mine, CTX, axis=0, tiled=False)

    latent = sent_to_all(q_latent.T, ("xh", "y")).reshape(QL, TOK)
    keys = jnp.concatenate([latent_cache.T, pos_rows], axis=0)
    keys = sent_to_all(keys, "z")

    absolute = (token_pos + start_offset[0]).astype(F32)
    freqs = rope_base ** (-jnp.arange(ROPE // 2, dtype=F32) * 2.0 / ROPE)
    angle = freqs[:, None] * absolute[None, :]
    query = kernel_call(
        query_body,
        (QROWS, TOK),
        (latent, w_q_up.T, jnp.cos(angle), jnp.sin(angle), pos_rows),
        flops=300_000_000,
    )
    queries = lax.all_gather(query, NEAR, axis=0, tiled=False)

    per_head = w_kv_up.reshape(KVL, HEADS, NOPE + VDIM)
    w_key = per_head[:, :, :NOPE].reshape(KVL, HEADS * NOPE)
    w_value_t = per_head[:, :, NOPE:].reshape(KVL, HEADS * VDIM).T
    count = keys.shape[0] * TOK
    parts = kernel_call(
        attend_body,
        (4, OROWS, TOK),
        (queries, keys, w_key, w_value_t),
        scratch=(
            pltpu.VMEM((count, KVL), BF16),
            pltpu.VMEM((count, ROPE), BF16),
            pltpu.VMEM((count, 1), F32),
            pltpu.VMEM((HEADS, count, QD), BF16),
            pltpu.VMEM((HEADS * VDIM, count), BF16),
        ),
        flops=3_500_000_000,
    )
    parts = lax.all_to_all(parts, NEAR, split_axis=0, concat_axis=0, tiled=True)
    mine = kernel_call(merge_body, (HEADS * VDIM, TOK), (parts,), flops=1_000_000)
    both = lax.all_gather(mine, "xh", axis=0, tiled=False)

    w_all = w_all.reshape(2, -1, HEADS * VDIM)
    partial = project(w_all, both, 8)
    partial = partial.reshape(8, -1, TOK)
    arrived = lax.all_to_all(partial, "y", split_axis=0, concat_axis=0, tiled=True)
    return arrived.astype(F32).sum(axis=0).astype(BF16).T


def solution(mesh):
    fine = Mesh(mesh.devices.reshape(8, 2, 2, 2, 8), ("z", "xl", "core", "xh", "y"))
    head = ("xh", "y")
    in_specs = (
        P(CTX, head),
        P(CTX, None),
        P(None, head),
        P(None, head),
        P(head, CTX),
        P(CTX),
        P(),
    )
    return jax.shard_map(
        shards, mesh=fine, in_specs=in_specs, out_specs=P(CTX, head), check_vma=False
    )
```

time: 240 us -> 187 us (0.78)
  waiting for transfers between devices: 71.1 us -> 29.3 us
  starting transfers between devices: 10.3 us -> 38.8 us
  blocking collectives: 93.5 us -> 66.4 us
  Pallas kernels: 0 us -> 23.3 us
  matrix products: 20.4 us -> 0 us
  local copies, waits for them, and re-layouts: 23.4 us -> 10.1 us
    all_gather x2 -> x1, waiting for transfers between devices: 69.7 us -> 0.01 us  [shards(): w_all = lax.all_gather(w_mine, CTX, axis=0, tiled=False)]
    all_to_all x1 -> x2, waiting for transfers between devices: 0.01 us -> 29.3 us  [sent_to_all(): return lax.all_to_all(copies, axis, split_axis=0, concat_axis=0, tiled=True)]
    all_to_all x1 -> x2, starting transfers between devices: 10.3 us -> 37.2 us  [sent_to_all(): return lax.all_to_all(copies, axis, split_axis=0, concat_axis=0, tiled=True)]
    pallas_call x0 -> x4, Pallas kernels: none -> 23.3 us  [the longest x3 15.3 us: kernel_call(): pl.pallas_call(body, out_shape=jax.ShapeDtypeStruct(shape, BF16), in_spec...]
    dot_general x28 -> x0, matrix products: 20.4 us -> none  [the longest x1 5.58 us: shards(): jnp.dot(attention, lax.all_gather(w_out, 'ctx', axis=1, tiled=True), pref...]
    all_gather x1 -> x2, blocking collectives: 39.9 us -> 21.3 us  [the longest x1 13.2 us: shards(): queries = lax.all_gather(query, NEAR, axis=0, tiled=False)]
    squeeze x8 -> x0, local copies, waits for them, and re-layouts: 8.87 us -> none  [shards(): lax.scan(scan_step, carry, (block.reshape(count, 512, block.shape[1]), ke...]
    all_to_all x1 -> x2, blocking collectives: 53.5 us -> 45.1 us  [the longest x1 29.7 us: shards(): lax.all_to_all(partial, 'y', split_axis=0, concat_axis=0, tiled=True)]
  transfers between devices with their start and end apart: 3 -> 4, of which waited for: 2 -> 2; matrix products, arithmetic and copies ran while one was open for 17% -> 7% of each run, Pallas kernels for 0% -> 8%
where the time goes in v1:
time: 187 us; the launch traced here: 186 us
  blocking collectives  66.4 us (36%)
  starting transfers between devices  38.8 us (21%)
  waiting for transfers between devices  29.3 us (16%)
  Pallas kernels  23.3 us (12%)
  between operations  14.1 us (8%)
  local copies, waits for them, and re-layouts  10.1 us (5%)
  other arithmetic  3.73 us (2%)
    all_to_all x2, starting transfers between devices, sent_to_all(): return lax.all_to_all(copies, axis, split_axis=0, concat_axis=0, tiled=True)  37.2 us
    all_to_all x1, blocking collectives, shards(): lax.all_to_all(partial, 'y', split_axis=0, concat_axis=0, tiled=True)  29.7 us
    all_to_all x2, waiting for transfers between devices, sent_to_all(): return lax.all_to_all(copies, axis, split_axis=0, concat_axis=0, tiled=True)  29.3 us
    all_to_all x1, blocking collectives, shards(): parts = lax.all_to_all(parts, NEAR, split_axis=0, concat_axis=0, tiled=True)  15.4 us
    pallas_call x3, Pallas kernels, kernel_call(): pl.pallas_call(body, out_shape=jax.ShapeDtypeStruct(shape, BF16), in_spec...  15.3 us
    all_gather x1, blocking collectives, shards(): queries = lax.all_gather(query, NEAR, axis=0, tiled=False)  13.2 us
    all_gather x1, blocking collectives, shards(): both = lax.all_gather(mine, 'xh', axis=0, tiled=False)  8.12 us
    pallas_call x1, Pallas kernels, project(): pl.pallas_call(project_body, grid=(tiles,), out_shape=jax.ShapeDtypeStruc...  8.01 us
  transfers between devices with their start and end apart: 4, of which 2 were waited for; matrix products, arithmetic and copies ran while one was open for 7% of the time, Pallas kernels for 8%

profile of v1, /device:TPU:1, one launch (start us, length us, event | category | flops | bytes accessed | tf_op | source)
XLA Modules:
  0.0 185.8 jit_solution(5087727432184171086)
XLA Ops:
  6.5 0.0 all-gather.5.cloned.1.call-start
  6.5 1.6 collective-permute-start
  8.1 0.0 collective-permute-done
  8.1 0.0 copy-start.2
  8.1 0.7 copy-done.2
  8.8 0.0 all-gather.5.cloned.1.call-update
  8.8 1.5 broadcast_in_dim.19
  10.4 0.0 copy-start
  10.4 24.9 %all-to-all-start = ((bf16[16,96,128]{2,1,0:T(8,128)(2,1)}), bf16[16,96,128]{2,1,0:T(8,128)(2,1)S(1)}, u32[]{:S(2)}, u32[]{:S(2)}) async-start(bf16[16,96,128]{2,1,0:T(8,128)(2,1)} %broadcast_in_dim.19), calls=%async_computation | async-start | bytes 786432 | tf_op jit(solution)/shard_map/all_to_all | solution.py:149
  35.9 0.7 convert_bitcast_fusion.1
  36.5 0.9 pad_maximum_fusion
  37.5 10.1 %all-to-all-done = bf16[16,96,128]{2,1,0:T(8,128)(2,1)S(1)} async-done(((bf16[16,96,128]{2,1,0:T(8,128)(2,1)}), bf16[16,96,128]{2,1,0:T(8,128)(2,1)S(1)}, u32[]{:S(2)}, u32[]{:S(2)}) %all-to-all-start) | async-done | bytes 393248 | tf_op jit(solution)/shard_map/all_to_all | solution.py:149
  47.6 0.0 copy-start.1
  47.6 1.2 broadcast_in_dim.23
  48.8 12.4 %all-to-all-start.1 = ((bf16[8,592,128]{2,1,0:T(8,128)(2,1)}), bf16[8,592,128]{2,1,0:T(8,128)(2,1)}, u32[]{:S(2)}, u32[]{:S(2)}) async-start(bf16[8,592,128]{2,1,0:T(8,128)(2,1)} %broadcast_in_dim.23), calls=%async_computation.1 | async-start | bytes 2424832 | tf_op jit(solution)/shard_map/all_to_all | solution.py:149
  61.2 0.0 copy-done
  61.2 2.5 %copy.8 = bf16[1536,768]{0,1:T(8,128)(2,1)} copy(bf16[1536,768]{1,0:T(8,128)(2,1)S(1)} %copy-done) | data formatting | bytes 4718592 | tf_op args[2]
  63.6 0.0 copy-done.1
  63.7 1.9 %reshape.27 = bf16[512,4,256]{2,1,0:T(4,128)(2,1)S(1)} reshape(bf16[512,1024]{1,0:T(8,128)(2,1)} %param.10) | data formatting | bytes 2097152 | tf_op jit(solution)/shard_map/reshape | solution.py:185
  65.5 0.4 fusion
  65.9 1.2 copy.10
  67.0 0.9 copy.13
  67.9 0.6 pad_maximum_fusion.1.pos
  68.5 0.7 multiply_sine_fusion
  69.3 3.2 %shard_map.73 = bf16[784,128]{1,0:T(8,128)(2,1)} custom-call(bf16[1536,128]{1,0:T(8,128)(2,1)} %bitcast.27, bf16[768,1536]{1,0:T(8,128)(2,1)} %bitcast.23, f32[32,128]{1,0:T(8,128)} %get-tuple-element.8.cosine, f32[32,128]{1,0:T(8,128)} %get-tuple-element.7.sine, bf16[16,128]{1,0:T(8,128)(2,1)} %pad_maximum_fusion.1.pos), custom_call_target="tpu_custom_call" | custom-call | flops 300000000 | bytes 4000000 | tf_op jit(solution)/shard_map/pallas_call | solution.py:38
  72.5 13.2 %all-gather.1 = bf16[3136,128]{1,0:T(8,128)(2,1)} all-gather(bf16[784,128]{1,0:T(8,128)(2,1)} %shard_map.73), channel_id=3, replica_groups=mesh['z'=8,'xl'=2,'core'=2,'xh'=2,'y'=8] {'xl','core'}, dimensions={0}, use_global_device_ids=true | all-gather | bytes 1003520 | tf_op jit(solution)/shard_map/all_gather | solution.py:183
  85.7 19.1 %all-to-all-done.1.keys = bf16[8,592,128]{2,1,0:T(8,128)(2,1)} async-done(((bf16[8,592,128]{2,1,0:T(8,128)(2,1)}), bf16[8,592,128]{2,1,0:T(8,128)(2,1)}, u32[]{:S(2)}, u32[]{:S(2)}) %all-to-all-start.1) | async-done | bytes 1212448 | tf_op jit(solution)/shard_map/all_to_all | solution.py:149
  104.9 10.2 %shard_map.74 = bf16[4,528,128]{2,1,0:T(8,128)(2,1)} custom-call(bf16[4,784,128]{2,1,0:T(8,128)(2,1)} %bitcast.29, bf16[8,592,128]{2,1,0:T(8,128)(2,1)} %all-to-all-done.1.keys, bf16[512,512]{1,0:T(8,128)(2,1)} %bitcast.31, bf16[512,512]{1,0:T(8,128)(2,1)} %bitcast.30), custom_call_target="tpu_custom_call" | custom-call | flops 3500000000 | bytes 4000000 | tf_op jit(solution)/shard_map/pallas_call | solution.py:38
  115.1 15.4 %all_to_all.20.parts = bf16[4,528,128]{2,1,0:T(8,128)(2,1)} all-to-all(bf16[4,528,128]{2,1,0:T(8,128)(2,1)} %shard_map.74), channel_id=1, replica_groups=mesh['z'=8,'xl'=2,'core'=2,'xh'=2,'y'=8] {'xl','core'}, dimensions={0} | all-to-all | bytes 1081344 | tf_op jit(solution)/shard_map/all_to_all | solution.py:202
  130.4 1.9 shard_map.75
  132.3 8.1 %all-gather.2 = bf16[1024,128]{1,0:T(8,128)(2,1)} all-gather(bf16[512,128]{1,0:T(8,128)(2,1)} %shard_map.75), channel_id=4, replica_groups=mesh['z'=8,'xl'=2,'core'=2,'xh'=2,'y'=8] {'xh'}, dimensions={0}, use_global_device_ids=true | all-gather | bytes 393216 | tf_op jit(solution)/shard_map/all_gather | solution.py:204
  140.4 0.0 all-gather.5.cloned.1.call-done
  140.4 8.0 %shard_map.76 = bf16[3584,128]{1,0:T(8,128)(2,1)} custom-call(bf16[2,3584,512]{2,1,0:T(8,128)(2,1)} %bitcast.24, bf16[2,512,128]{2,1,0:T(8,128)(2,1)} %bitcast.28), custom_call_target="tpu_custom_call" | custom-call | flops 939524096 | bytes 8000000 | tf_op jit(solution)/shard_map/pallas_call | solution.py:131
  148.4 29.7 %all_to_all.21 = bf16[8,448,128]{2,1,0:T(8,128)(2,1)S(1)} all-to-all(bf16[8,448,128]{2,1,0:T(8,128)(2,1)} %bitcast.25), channel_id=1, replica_groups=mesh['z'=8,'xl'=2,'core'=2,'xh'=2,'y'=8] {'y'}, dimensions={0} | all-to-all | bytes 1835008 | tf_op jit(solution)/shard_map/all_to_all | solution.py:209
  178.1 0.8 reduce_sum.12
  (2 shorter events, 0.0 us)
Async XLA Ops:
  6.5 133.9 %all-gather.5.cloned.1.call-start = ((), (), s32[]{:S(2)}) async-start(), calls=%async_computation.4 | async-start | bytes 7569408 | tf_op jit(solution)/shard_map/all_gather | solution.py:168
  6.5 1.6 collective-permute-start
  8.1 0.7 copy-start.2
  10.4 50.8 %copy-start = (bf16[1536,768]{1,0:T(8,128)(2,1)S(1)}, bf16[1536,768]{1,0:T(8,128)(2,1)}, u32[]{:S(2)}) copy-start(bf16[1536,768]{1,0:T(8,128)(2,1)} %param.9) | copy-start | bytes 7077892
  10.4 37.2 %all-to-all-start = ((bf16[16,96,128]{2,1,0:T(8,128)(2,1)}), bf16[16,96,128]{2,1,0:T(8,128)(2,1)S(1)}, u32[]{:S(2)}, u32[]{:S(2)}) async-start(bf16[16,96,128]{2,1,0:T(8,128)(2,1)} %broadcast_in_dim.19), calls=%async_computation | async-start | bytes 786432 | tf_op jit(solution)/shard_map/all_to_all | solution.py:149
  47.6 16.1 %copy-start.1 = (bf16[16,96,128]{2,1,0:T(8,128)(2,1)}, bf16[16,96,128]{2,1,0:T(8,128)(2,1)S(1)}, u32[]{:S(2)}) copy-start(bf16[16,96,128]{2,1,0:T(8,128)(2,1)S(1)} %all-to-all-done) | copy-start | bytes 1179652
  48.8 56.1 %all-to-all-start.1 = ((bf16[8,592,128]{2,1,0:T(8,128)(2,1)}), bf16[8,592,128]{2,1,0:T(8,128)(2,1)}, u32[]{:S(2)}, u32[]{:S(2)}) async-start(bf16[8,592,128]{2,1,0:T(8,128)(2,1)} %broadcast_in_dim.23), calls=%async_computation.1 | async-start | bytes 2424832 | tf_op jit(solution)/shard_map/all_to_all | solution.py:149
Sparse Core Ops, SparseCore 0:
  9.5 116.3 all-gather.4

commit v2 on v1

--- a/solution.py
+++ b/solution.py
@@ -1,3 +1,5 @@
+import itertools
+
 import jax
 import jax.numpy as jnp
 from jax import lax
@@ -24,7 +26,7 @@
 
 F32 = jnp.float32
 BF16 = jnp.bfloat16
-CTX = ("z", "xl", "core")
+CTX = ("za", "zb", "xl", "core")
 NEAR = ("xl", "core")
 VMEM = pl.BlockSpec(memory_space=pltpu.VMEM)
 LIMIT = 56 * 1024 * 1024
@@ -122,26 +124,35 @@
         out[rows, :] = (added / whole).astype(BF16)
 
 
-def project_body(w, x, out):
-    out[...] = (dot(w[0], x[0]) + dot(w[1], x[1])).astype(BF16)
-
-
-def project(w, x, tiles):
-    rows = w.shape[1] // tiles
+def project_body(w, mine, theirs, place, out):
+    total = 0.0
+    rows = w.shape[0] * w.shape[2]
+    for g in range(4):
+        group = place[0] ^ g
+        tokens = jnp.concatenate([mine[group], theirs[group]], axis=1)
+        total = total + dot(w[:, g].reshape(rows, w.shape[3]), tokens)
+    out[...] = total.astype(BF16).reshape(out.shape)
+
+
+def project(w, mine, theirs, place):
+    tiles, _, rows, depth = w.shape
+    wide = 2 * TOK
     return pl.pallas_call(
         project_body,
-        grid=(tiles,),
-        out_shape=jax.ShapeDtypeStruct((w.shape[1], TOK), BF16),
+        grid=(tiles // 2,),
+        out_shape=jax.ShapeDtypeStruct((tiles, rows, wide), BF16),
         in_specs=[
-            pl.BlockSpec((2, rows, w.shape[2]), lambda i: (0, i, 0)),
-            pl.BlockSpec((2, x.shape[1], TOK), lambda i: (0, 0, 0)),
+            pl.BlockSpec((2, 4, rows, depth), lambda i: (i, 0, 0, 0)),
+            pl.BlockSpec(mine.shape, lambda i: (0, 0, 0)),
+            pl.BlockSpec(mine.shape, lambda i: (0, 0, 0)),
+            pl.BlockSpec(memory_space=pltpu.SMEM),
         ],
-        out_specs=pl.BlockSpec((rows, TOK), lambda i: (i, 0)),
+        out_specs=pl.BlockSpec((2, rows, wide), lambda i: (i, 0, 0)),
         compiler_params=pltpu.CompilerParams(vmem_limit_bytes=LIMIT),
         cost_estimate=pl.CostEstimate(
-            flops=4 * w.shape[1] * w.shape[2] * TOK, bytes_accessed=8_000_000, transcendentals=0
+            flops=8 * tiles * rows * depth * wide, bytes_accessed=5_000_000, transcendentals=0
         ),
-    )(w, x)
+    )(w, mine, theirs, place)
 
 
 def sent_to_all(array, axis):
@@ -149,13 +160,10 @@
     return lax.all_to_all(copies, axis, split_axis=0, concat_axis=0, tiled=True)
 
 
-def crossed():
+def crossed(half, flip):
     pairs = []
-    for z in range(8):
-        for xh in range(2):
-            source = z * 2 + xh
-            target = source if z // 4 == xh else (z ^ 4) * 2 + (1 - xh)
-            pairs.append((source, target))
+    for b, c, d in itertools.product(range(2), repeat=3):
+        pairs.append(((b * 2 + c) * 2 + d, ((d ^ flip) * 2 + (c ^ half)) * 2 + b))
     return pairs
 
 
@@ -164,12 +172,19 @@
         [(token_pos >> 6)[None], (token_pos & 63)[None], jnp.zeros((14, TOK), jnp.int32)], axis=0
     ).astype(BF16)
 
-    w_mine = lax.ppermute(w_out.T, ("z", "xh"), crossed())
-    w_all = lax.all_gather(w_mine, CTX, axis=0, tiled=False)
-
-    latent = sent_to_all(q_latent.T, ("xh", "y")).reshape(QL, TOK)
+    columns = w_out.T.reshape(2, -1, HEADS * VDIM)
+    xh = lax.axis_index("xh")
+    halves = [lax.dynamic_index_in_dim(columns, xh ^ half, 0, keepdims=False) for half in range(2)]
+    w_mine = [
+        lax.ppermute(halves[half], ("xl", "xh", "yl"), crossed(half, flip))
+        for half in range(2)
+        for flip in range(2)
+    ]
     keys = jnp.concatenate([latent_cache.T, pos_rows], axis=0)
-    keys = sent_to_all(keys, "z")
+    keys = lax.all_gather(keys, ("za", "zb"), axis=0, tiled=False)
+    latent = sent_to_all(q_latent.T, ("xh", "yh", "yl")).reshape(QL, TOK)
+    latent, w_mine = lax.optimization_barrier((latent, w_mine))
+    w_all = lax.all_gather(jnp.stack(w_mine), ("za", "zb"), axis=0, tiled=False)
 
     absolute = (token_pos + start_offset[0]).astype(F32)
     freqs = rope_base ** (-jnp.arange(ROPE // 2, dtype=F32) * 2.0 / ROPE)
@@ -201,18 +216,22 @@
     )
     parts = lax.all_to_all(parts, NEAR, split_axis=0, concat_axis=0, tiled=True)
     mine = kernel_call(merge_body, (HEADS * VDIM, TOK), (parts,), flops=1_000_000)
-    both = lax.all_gather(mine, "xh", axis=0, tiled=False)
-
-    w_all = w_all.reshape(2, -1, HEADS * VDIM)
-    partial = project(w_all, both, 8)
-    partial = partial.reshape(8, -1, TOK)
-    arrived = lax.all_to_all(partial, "y", split_axis=0, concat_axis=0, tiled=True)
-    return arrived.astype(F32).sum(axis=0).astype(BF16).T
+    mine = lax.all_gather(mine, ("xh", "yl"), axis=0, tiled=False)
+    theirs = lax.ppermute(mine, "core", [(0, 1), (1, 0)])
+    place = (xh * 2 + lax.axis_index("xl")).astype(jnp.int32)[None]
+    partial = project(w_all, mine, theirs, place)
+    arrived = lax.all_to_all(partial, ("xh", "yh"), split_axis=0, concat_axis=0, tiled=True)
+    arrived = arrived.reshape(2, 4, -1, 2 * TOK)
+    summed = arrived.astype(F32).sum(axis=1).astype(BF16).reshape(-1, 2 * TOK)
+    kept = summed[:, :TOK]
+    got = lax.ppermute(summed[:, TOK:], "core", [(0, 1), (1, 0)])
+    first = lax.axis_index("core") == 0
+    return jnp.concatenate([jnp.where(first, kept, got), jnp.where(first, got, kept)], axis=0).T
 
 
 def solution(mesh):
-    fine = Mesh(mesh.devices.reshape(8, 2, 2, 2, 8), ("z", "xl", "core", "xh", "y"))
-    head = ("xh", "y")
+    fine = Mesh(mesh.devices.reshape(2, 4, 2, 2, 2, 4, 2), ("za", "zb", "xl", "core", "xh", "yh", "yl"))
+    head = ("xh", "yh", "yl")
     in_specs = (
         P(CTX, head),
         P(CTX, None),

time: 187 us -> 154 us (0.82)
  waiting for transfers between devices: 29.3 us -> 10.9 us
  blocking collectives: 66.4 us -> 59.8 us
  starting transfers between devices: 38.8 us -> 33.2 us
  Pallas kernels: 23.3 us -> 20 us
    all_to_all x2 -> x1, waiting for transfers between devices: 29.3 us -> 0.01 us  [sent_to_all(): return lax.all_to_all(copies, axis, split_axis=0, concat_axis=0, tiled=True)]
    all_to_all x2 -> x1, starting transfers between devices: 37.2 us -> 10.2 us  [sent_to_all(): return lax.all_to_all(copies, axis, split_axis=0, concat_axis=0, tiled=True)]
    ppermute x1 -> x6, starting transfers between devices: 1.58 us -> 22.9 us  [the longest x4 12.9 us: shards(): lax.ppermute(halves[half], ('xl', 'xh', 'yl'), crossed(half, flip))]
    ppermute x1 -> x6, waiting for transfers between devices: 0.01 us -> 10.8 us  [the longest x4 8.46 us: shards(): lax.ppermute(halves[half], ('xl', 'xh', 'yl'), crossed(half, flip))]
    all_to_all x1, blocking collectives: 29.7 us -> 23.6 us  [shards(): lax.all_to_all(partial, ('xh', 'yh'), split_axis=0, concat_axis=0, tiled=...]
    all_gather x1, blocking collectives: 8.12 us -> 13.7 us  [shards(): mine = lax.all_gather(mine, ('xh', 'yl'), axis=0, tiled=False)]
    all_gather x1, blocking collectives: 13.2 us -> 9.45 us  [shards(): queries = lax.all_gather(query, NEAR, axis=0, tiled=False)]
    pallas_call x1, Pallas kernels: 8.01 us -> 4.84 us  [project(): pl.pallas_call(project_body, grid=(tiles // 2,), out_shape=jax.ShapeDtype...]
  transfers between devices with their start and end apart: 4 -> 9, of which waited for: 2 -> 5; matrix products, arithmetic and copies ran while one was open for 7% -> 8% of each run, Pallas kernels for 8% -> 10%
where the time goes in v2:
time: 154 us; the launch traced here: 153 us
  blocking collectives  59.8 us (39%)
  starting transfers between devices  33.2 us (22%)
  Pallas kernels  20 us (13%)
  between operations  14.3 us (9%)
  waiting for transfers between devices  10.9 us (7%)
  local copies, waits for them, and re-layouts  10.1 us (7%)
  other arithmetic  5.32 us (3%)
    all_to_all x1, blocking collectives, shards(): lax.all_to_all(partial, ('xh', 'yh'), split_axis=0, concat_axis=0, tiled=...  23.6 us
    pallas_call x3, Pallas kernels, kernel_call(): pl.pallas_call(body, out_shape=jax.ShapeDtypeStruct(shape, BF16), in_spec...  15.1 us
    all_gather x1, blocking collectives, shards(): mine = lax.all_gather(mine, ('xh', 'yl'), axis=0, tiled=False)  13.7 us
    all_to_all x1, blocking collectives, shards(): parts = lax.all_to_all(parts, NEAR, split_axis=0, concat_axis=0, tiled=True)  13 us
    ppermute x4, starting transfers between devices, shards(): lax.ppermute(halves[half], ('xl', 'xh', 'yl'), crossed(half, flip))  12.9 us
    all_to_all x1, starting transfers between devices, sent_to_all(): return lax.all_to_all(copies, axis, split_axis=0, concat_axis=0, tiled=True)  10.2 us
    all_gather x1, blocking collectives, shards(): queries = lax.all_gather(query, NEAR, axis=0, tiled=False)  9.45 us
    ppermute x4, waiting for transfers between devices, shards(): lax.ppermute(halves[half], ('xl', 'xh', 'yl'), crossed(half, flip))  8.46 us
  transfers between devices with their start and end apart: 9, of which 5 were waited for; matrix products, arithmetic and copies ran while one was open for 8% of the time, Pallas kernels for 10%

profile of v2, /device:TPU:1, one launch (start us, length us, event | category | flops | bytes accessed | tf_op | source)
XLA Modules:
  0.0 153.5 jit_solution(12668184968233253331)
XLA Ops:
  6.5 0.0 copy-start
  6.5 0.0 all-gather.9.cloned.1.call-start
  7.3 0.7 convert_bitcast_fusion.1
  8.0 1.6 %pad_maximum_fusion.1 = bf16[592,128]{1,0:T(8,128)(2,1)} fusion(bf16[14,128]{1,0:T(8,128)(2,1)S(1)} %broadcast_in_dim.22, bf16[1,128]{1,0:T(2,128)(2,1)S(1)} %get-tuple-element.25, bf16[1,128]{1,0:T(2,128)(2,1)S(1)} %get-tuple-element.23, bf16[576,128]{1,0:T(8,128)(2,1)} %bitcast.50), kind=kLoop, calls=%fused_computation.3 | loop fusion | flops 606208 | bytes 303104 | tf_op jit(solution)/shard_map/concatenate | solution.py:183
  9.6 0.0 all-gather.9.cloned.1.call-update
  9.6 1.5 %broadcast_in_dim.19 = bf16[16,96,128]{2,1,0:T(8,128)(2,1)} broadcast(bf16[96,128]{1,0:T(8,128)(2,1)} %bitcast.55), dimensions={1,2} | broadcast | bytes 417792 | tf_op jit(solution)/shard_map/broadcast_in_dim | solution.py:159
  11.2 10.2 %all-to-all-start = ((bf16[16,96,128]{2,1,0:T(8,128)(2,1)}), bf16[16,96,128]{2,1,0:T(8,128)(2,1)S(1)}, u32[]{:S(2)}, u32[]{:S(2)}) async-start(bf16[16,96,128]{2,1,0:T(8,128)(2,1)} %broadcast_in_dim.19), calls=%async_computation | async-start | bytes 786432 | tf_op jit(solution)/shard_map/all_to_all | solution.py:160
  21.4 0.0 all-gather.7.cloned.1.call-start
  21.4 1.0 dynamic-slice_bitcast_fusion
  22.4 0.7 collective-permute-start
  23.1 5.7 %collective-permute-start.1 = (bf16[112,512]{1,0:T(8,128)(2,1)S(1)}, bf16[112,512]{1,0:T(8,128)(2,1)S(1)}, u32[]{:S(2)}, u32[]{:S(2)}) collective-permute-start(bf16[112,512]{1,0:T(8,128)(2,1)S(1)} %get-tuple-element.18), channel_id=1, source_target_pairs={{0,32},{1,0},{8,40},{9,8},{32,33},{33,1},{40,41},{41,9},{2,34},{3,... | collective-permute-start | bytes 344072 | tf_op jit(solution)/shard_map/ppermute | solution.py:179
  28.8 4.6 %collective-permute-start.2 = (bf16[112,512]{1,0:T(8,128)(2,1)S(1)}, bf16[112,512]{1,0:T(8,128)(2,1)S(1)}, u32[]{:S(2)}, u32[]{:S(2)}) collective-permute-start(bf16[112,512]{1,0:T(8,128)(2,1)S(1)} %get-tuple-element.17), channel_id=1, source_target_pairs={{0,8},{1,40},{8,0},{9,32},{32,9},{33,41},{40,1},{41,33},{2,10},{3,... | collective-permute-start | bytes 344072 | tf_op jit(solution)/shard_map/ppermute | solution.py:179
  33.4 1.9 %collective-permute-start.3 = (bf16[112,512]{1,0:T(8,128)(2,1)S(1)}, bf16[112,512]{1,0:T(8,128)(2,1)S(1)}, u32[]{:S(2)}, u32[]{:S(2)}) collective-permute-start(bf16[112,512]{1,0:T(8,128)(2,1)S(1)} %get-tuple-element.17), channel_id=1, source_target_pairs={{0,40},{1,8},{8,32},{9,0},{32,41},{33,9},{40,33},{41,1},{2,42},{3,... | collective-permute-start | bytes 344072 | tf_op jit(solution)/shard_map/ppermute | solution.py:179
  35.3 0.0 collective-permute-done
  35.3 1.2 collective-permute-done.1
  36.5 4.3 %collective-permute-done.2 = bf16[112,512]{1,0:T(8,128)(2,1)S(1)} collective-permute-done((bf16[112,512]{1,0:T(8,128)(2,1)S(1)}, bf16[112,512]{1,0:T(8,128)(2,1)S(1)}, u32[]{:S(2)}, u32[]{:S(2)}) %collective-permute-start.2) | collective-permute-done | bytes 114720 | tf_op jit(solution)/shard_map/ppermute | solution.py:179
  40.8 3.0 %collective-permute-done.3 = bf16[112,512]{1,0:T(8,128)(2,1)S(1)} collective-permute-done((bf16[112,512]{1,0:T(8,128)(2,1)S(1)}, bf16[112,512]{1,0:T(8,128)(2,1)S(1)}, u32[]{:S(2)}, u32[]{:S(2)}) %collective-permute-start.3) | collective-permute-done | bytes 114720 | tf_op jit(solution)/shard_map/ppermute | solution.py:179
  43.8 0.0 all-to-all-done
  43.8 0.0 copy-start.2
  43.8 1.0 pad_maximum_fusion
  44.8 0.0 all-gather.7.cloned.1.call-update
  44.8 0.0 copy-done
  44.8 2.5 %copy.10 = bf16[1536,768]{0,1:T(8,128)(2,1)} copy(bf16[1536,768]{1,0:T(8,128)(2,1)S(1)} %copy-done) | data formatting | bytes 4718592 | tf_op args[2]
  47.3 0.0 copy-done.2
  47.3 1.9 %reshape.30 = bf16[512,4,256]{2,1,0:T(4,128)(2,1)S(1)} reshape(bf16[512,1024]{1,0:T(8,128)(2,1)} %param.10) | data formatting | bytes 2097152 | tf_op jit(solution)/shard_map/reshape | solution.py:200
  49.2 0.4 fusion
  49.5 1.1 copy.12
  50.7 0.9 copy.15
  51.6 0.6 pad_maximum_fusion.2.pos
  52.2 0.8 multiply_sine_fusion
  52.9 3.2 %shard_map.73 = bf16[784,128]{1,0:T(8,128)(2,1)} custom-call(bf16[1536,128]{1,0:T(8,128)(2,1)} %bitcast.43, bf16[768,1536]{1,0:T(8,128)(2,1)} %bitcast.38, f32[32,128]{1,0:T(8,128)} %get-tuple-element.22.cosine, f32[32,128]{1,0:T(8,128)} %get-tuple-element.21.sine, bf16[16,128]{1,0:T(8,128)(2,1)} %pad_maximum_fusion.2.pos), custom_call_target="tpu_custom_call" | custom-call | flops 300000000 | bytes 4000000 | tf_op jit(solution)/shard_map/pallas_call | solution.py:40
  56.1 9.5 %all-gather.1 = bf16[3136,128]{1,0:T(8,128)(2,1)} all-gather(bf16[784,128]{1,0:T(8,128)(2,1)} %shard_map.73), channel_id=3, replica_groups=mesh['za'=2,'zb'=4,'xl'=2,'core'=2,'xh'=2,'yh'=4,'yl'=2] {'xl','core'}, dimensions={0}, use_global_device_ids=true | all-gather | bytes 1003520 | tf_op jit(solution)/shard_map/all_gather | solution.py:198
  65.6 0.0 all-gather.9.cloned.1.call-done
  65.6 10.1 %shard_map.74 = bf16[4,528,128]{2,1,0:T(8,128)(2,1)} custom-call(bf16[4,784,128]{2,1,0:T(8,128)(2,1)} %bitcast.44, bf16[8,592,128]{2,1,0:T(8,128)(2,1)} %bitcast.56, bf16[512,512]{1,0:T(8,128)(2,1)} %bitcast.46, bf16[512,512]{1,0:T(8,128)(2,1)} %bitcast.45), custom_call_target="tpu_custom_call" | custom-call | flops 3500000000 | bytes 4000000 | tf_op jit(solution)/shard_map/pallas_call | solution.py:40
  75.7 13.0 %all_to_all.15.parts = bf16[4,528,128]{2,1,0:T(8,128)(2,1)} all-to-all(bf16[4,528,128]{2,1,0:T(8,128)(2,1)} %shard_map.74), channel_id=1, replica_groups=mesh['za'=2,'zb'=4,'xl'=2,'core'=2,'xh'=2,'yh'=4,'yl'=2] {'xl','core'}, dimensions={0} | all-to-all | bytes 1081344 | tf_op jit(solution)/shard_map/all_to_all | solution.py:217
  88.7 1.8 %shard_map.75 = bf16[512,128]{1,0:T(8,128)(2,1)} custom-call(bf16[4,528,128]{2,1,0:T(8,128)(2,1)} %all_to_all.15.parts), custom_call_target="tpu_custom_call" | custom-call | flops 1000000 | bytes 4000000 | tf_op jit(solution)/shard_map/pallas_call | solution.py:40
  90.5 13.7 %all-gather.3 = bf16[2048,128]{1,0:T(8,128)(2,1)S(1)} all-gather(bf16[512,128]{1,0:T(8,128)(2,1)} %shard_map.75), channel_id=5, replica_groups=mesh['za'=2,'zb'=4,'xl'=2,'core'=2,'xh'=2,'yh'=4,'yl'=2] {'xh','yl'}, dimensions={0}, use_global_device_ids=true | all-gather | bytes 655360 | tf_op jit(solution)/shard_map/all_gather | solution.py:219
  104.3 0.0 copy-start.1
  104.3 5.9 %collective-permute-start.4 = (bf16[4,512,128]{2,1,0:T(8,128)(2,1)S(1)}, bf16[4,512,128]{2,1,0:T(8,128)(2,1)S(1)}, u32[]{:S(2)}, u32[]{:S(2)}) collective-permute-start(bf16[4,512,128]{2,1,0:T(8,128)(2,1)S(1)} %bitcast.41), channel_id=1, source_target_pairs={{0,16},{16,0},{1,17},{17,1},{2,18},{18,2},{3,19},{19,3},{4,20},{20... | collective-permute-start | bytes 1572872 | tf_op jit(solution)/shard_map/ppermute | solution.py:220
  110.2 1.5 collective-permute-done.4.theirs
  111.7 0.0 copy-start.3
  111.7 0.0 all-gather.7.cloned.1.call-done
  111.7 0.0 copy-done.1
  111.7 0.8 copy-done.3
  112.5 4.8 %shard_map.76 = bf16[8,112,256]{2,1,0:T(8,128)(2,1)} custom-call(bf16[8,4,112,512]{3,2,1,0:T(8,128)(2,1)} %bitcast.39, bf16[4,512,128]{2,1,0:T(8,128)(2,1)} %bitcast.42, bf16[4,512,128]{2,1,0:T(8,128)(2,1)} %copy-done.3, s32[1]{0:T(128)} %bitcast.22.place), custom_call_target="tpu_custom_call" | custom-call | flops 939524096 | bytes 5000000 | tf_op jit(solution)/shard_map/pallas_call | solution.py:140
  117.3 23.6 %all_to_all.16 = bf16[8,112,256]{2,1,0:T(8,128)(2,1)S(1)} all-to-all(bf16[8,112,256]{2,1,0:T(8,128)(2,1)} %shard_map.76), channel_id=1, replica_groups=mesh['za'=2,'zb'=4,'xl'=2,'core'=2,'xh'=2,'yh'=4,'yl'=2] {'xh','yh'}, dimensions={0} | all-to-all | bytes 917504 | tf_op jit(solution)/shard_map/all_to_all | solution.py:223
  140.9 0.1 bitcast_reduce_fusion
  141.0 4.1 %collective-permute-start.5 = (bf16[224,128]{1,0:T(8,128)(2,1)S(1)}, bf16[224,128]{1,0:T(8,128)(2,1)S(1)}, u32[]{:S(2)}, u32[]{:S(2)}) collective-permute-start(bf16[224,128]{1,0:T(8,128)(2,1)S(1)} %slice.19), channel_id=1, source_target_pairs={{0,16},{16,0},{1,17},{17,1},{2,18},{18,2},{3,19},{19,3},{4,20},{20... | collective-permute-start | bytes 172040 | tf_op jit(solution)/shard_map/ppermute | solution.py:227
  145.1 0.9 collective-permute-done.5
  146.0 0.7 maximum_bitcast_fusion
  (4 shorter events, 0.0 us)
Async XLA Ops:
  6.5 38.3 %copy-start = (bf16[1536,768]{1,0:T(8,128)(2,1)S(1)}, bf16[1536,768]{1,0:T(8,128)(2,1)}, u32[]{:S(2)}) copy-start(bf16[1536,768]{1,0:T(8,128)(2,1)} %param.9) | copy-start | bytes 7077892
  6.5 59.0 %all-gather.9.cloned.1.call-start = ((), (), s32[]{:S(2)}) async-start(), calls=%async_computation.4 | async-start | bytes 1363968 | tf_op jit(solution)/shard_map/all_gather | solution.py:184
  11.2 32.6 %all-to-all-start = ((bf16[16,96,128]{2,1,0:T(8,128)(2,1)}), bf16[16,96,128]{2,1,0:T(8,128)(2,1)S(1)}, u32[]{:S(2)}, u32[]{:S(2)}) async-start(bf16[16,96,128]{2,1,0:T(8,128)(2,1)} %broadcast_in_dim.19), calls=%async_computation | async-start | bytes 786432 | tf_op jit(solution)/shard_map/all_to_all | solution.py:160
  21.4 90.3 %all-gather.7.cloned.1.call-start = ((), (), s32[]{:S(2)}) async-start(), calls=%async_computation.3 | async-start | bytes 4128768 | tf_op jit(solution)/shard_map/all_gather | solution.py:187
  22.4 12.9 %collective-permute-start = (bf16[112,512]{1,0:T(8,128)(2,1)S(1)}, bf16[112,512]{1,0:T(8,128)(2,1)S(1)}, u32[]{:S(2)}, u32[]{:S(2)}) collective-permute-start(bf16[112,512]{1,0:T(8,128)(2,1)S(1)} %get-tuple-element.18), channel_id=1, source_target_pairs={{0,0},{1,32},{8,8},{9,40},{32,1},{33,33},{40,9},{41,41},{2,2},{3,3... | collective-permute-start | bytes 344072 | tf_op jit(solution)/shard_map/ppermute | solution.py:179
  23.1 13.4 %collective-permute-start.1 = (bf16[112,512]{1,0:T(8,128)(2,1)S(1)}, bf16[112,512]{1,0:T(8,128)(2,1)S(1)}, u32[]{:S(2)}, u32[]{:S(2)}) collective-permute-start(bf16[112,512]{1,0:T(8,128)(2,1)S(1)} %get-tuple-element.18), channel_id=1, source_target_pairs={{0,32},{1,0},{8,40},{9,8},{32,33},{33,1},{40,41},{41,9},{2,34},{3,... | collective-permute-start | bytes 344072 | tf_op jit(solution)/shard_map/ppermute | solution.py:179
  28.8 12.0 %collective-permute-start.2 = (bf16[112,512]{1,0:T(8,128)(2,1)S(1)}, bf16[112,512]{1,0:T(8,128)(2,1)S(1)}, u32[]{:S(2)}, u32[]{:S(2)}) collective-permute-start(bf16[112,512]{1,0:T(8,128)(2,1)S(1)} %get-tuple-element.17), channel_id=1, source_target_pairs={{0,8},{1,40},{8,0},{9,32},{32,9},{33,41},{40,1},{41,33},{2,10},{3,... | collective-permute-start | bytes 344072 | tf_op jit(solution)/shard_map/ppermute | solution.py:179
  33.4 10.4 %collective-permute-start.3 = (bf16[112,512]{1,0:T(8,128)(2,1)S(1)}, bf16[112,512]{1,0:T(8,128)(2,1)S(1)}, u32[]{:S(2)}, u32[]{:S(2)}) collective-permute-start(bf16[112,512]{1,0:T(8,128)(2,1)S(1)} %get-tuple-element.17), channel_id=1, source_target_pairs={{0,40},{1,8},{8,32},{9,0},{32,41},{33,9},{40,33},{41,1},{2,42},{3,... | collective-permute-start | bytes 344072 | tf_op jit(solution)/shard_map/ppermute | solution.py:179
  43.8 3.5 %copy-start.2 = (bf16[16,96,128]{2,1,0:T(8,128)(2,1)}, bf16[16,96,128]{2,1,0:T(8,128)(2,1)S(1)}, u32[]{:S(2)}) copy-start(bf16[16,96,128]{2,1,0:T(8,128)(2,1)S(1)} %all-to-all-done) | copy-start | bytes 1179652
  104.3 7.5 %copy-start.1 = (bf16[2048,128]{1,0:T(8,128)(2,1)}, bf16[2048,128]{1,0:T(8,128)(2,1)S(1)}, u32[]{:S(2)}) copy-start(bf16[2048,128]{1,0:T(8,128)(2,1)S(1)} %all-gather.3) | copy-start | bytes 1572868
  104.3 7.4 %collective-permute-start.4 = (bf16[4,512,128]{2,1,0:T(8,128)(2,1)S(1)}, bf16[4,512,128]{2,1,0:T(8,128)(2,1)S(1)}, u32[]{:S(2)}, u32[]{:S(2)}) collective-permute-start(bf16[4,512,128]{2,1,0:T(8,128)(2,1)S(1)} %bitcast.41), channel_id=1, source_target_pairs={{0,16},{16,0},{1,17},{17,1},{2,18},{18,2},{3,19},{19,3},{4,20},{20... | collective-permute-start | bytes 1572872 | tf_op jit(solution)/shard_map/ppermute | solution.py:220
  111.7 0.8 copy-start.3
  141.0 5.0 %collective-permute-start.5 = (bf16[224,128]{1,0:T(8,128)(2,1)S(1)}, bf16[224,128]{1,0:T(8,128)(2,1)S(1)}, u32[]{:S(2)}, u32[]{:S(2)}) collective-permute-start(bf16[224,128]{1,0:T(8,128)(2,1)S(1)} %slice.19), channel_id=1, source_target_pairs={{0,16},{16,0},{1,17},{17,1},{2,18},{18,2},{3,19},{19,3},{4,20},{20... | collective-permute-start | bytes 172040 | tf_op jit(solution)/shard_map/ppermute | solution.py:227
Sparse Core Ops, SparseCore 0:
  9.7 44.0 all-gather.8
  56.0 55.2 all-gather.6

commit v3 on v2

--- a/solution.py
+++ b/solution.py
@@ -1,4 +1,5 @@
 import itertools
+import math
 
 import jax
 import jax.numpy as jnp
@@ -20,6 +21,7 @@
 OROWS = HEADS * VDIM + 16
 
 softmax_scale = 0.135
+scale = softmax_scale * math.log2(math.e)
 rope_base = 10000.0
 masked = -1e30
 floor = -1e29
@@ -36,20 +38,41 @@
     return jnp.dot(a, b, preferred_element_type=F32)
 
 
-def kernel_call(body, shape, args, scratch=(), flops=0):
+def kernel_call(body, shapes, args, scratch=(), flops=0, specs=None):
+    single = isinstance(shapes, tuple)
+    outs = [jax.ShapeDtypeStruct(shape, BF16) for shape in ([shapes] if single else shapes)]
     return pl.pallas_call(
         body,
-        out_shape=jax.ShapeDtypeStruct(shape, BF16),
-        in_specs=[VMEM] * len(args),
-        out_specs=VMEM,
+        out_shape=outs[0] if single else outs,
+        in_specs=specs or [VMEM] * len(args),
+        out_specs=VMEM if single else [VMEM] * len(outs),
         scratch_shapes=list(scratch),
         compiler_params=pltpu.CompilerParams(vmem_limit_bytes=LIMIT),
         cost_estimate=pl.CostEstimate(flops=flops, bytes_accessed=4_000_000, transcendentals=0),
     )(*args)
 
 
+def position_rows(pos):
+    row = lax.broadcasted_iota(jnp.int32, (16, TOK), 0)
+    pos = jnp.broadcast_to(pos, (16, TOK))
+    return jnp.where(row == 0, pos >> 6, jnp.where(row == 1, pos & 63, 0)).astype(F32).astype(BF16)
+
+
+def pack_body(latent, pos, out):
+    out[: KVL + ROPE, :] = latent[...]
+    out[KVL + ROPE :, :] = position_rows(pos[...])
+
+
+def weights_body(w, w_key, w_value_t):
+    for h in range(HEADS):
+        base = h * (NOPE + VDIM)
+        cols = slice(h * NOPE, (h + 1) * NOPE)
+        w_key[:, cols] = w[:, base : base + NOPE]
+        w_value_t[cols, :] = w[:, base + NOPE : base + NOPE + VDIM].T
+
+
 def query_body(latent, weights, cosine, sine, pos, out):
-    query = dot(weights[...], latent[...])
+    query = dot(latent[...].T, weights[...]).T
     cos, sin = cosine[...], sine[...]
     half = ROPE // 2
     for h in range(HEADS):
@@ -60,7 +83,7 @@
         out[base + NOPE : base + QD, :] = jnp.concatenate(
             [a * cos - b * sin, a * sin + b * cos], axis=0
         ).astype(BF16)
-    out[HEADS * QD :, :] = pos[...]
+    out[HEADS * QD :, :] = position_rows(pos[...])
 
 
 def attend_body(queries, keys, w_key, w_value_t, out, latent, rope_keys, key_pos, key_cat, value_t):
@@ -88,14 +111,14 @@
         stats = []
         for h in range(HEADS):
             q = jnp.concatenate([queries[t, h * QD : (h + 1) * QD, :] for t in two], axis=1)
-            scores = jnp.where(visible, dot(key_cat[h], q) * softmax_scale, masked)
+            scores = jnp.where(visible, dot(key_cat[h], q) * scale, masked)
             largest = jnp.maximum(jnp.max(scores, axis=0, keepdims=True), floor)
-            weights = jnp.exp(scores - largest)
+            weights = jnp.exp2(scores - largest)
             total = jnp.sum(weights, axis=0, keepdims=True)
             some = total > 0.0
             safe = jnp.where(some, total, 1.0)
             summed = dot(value_t[h * VDIM : (h + 1) * VDIM, :], weights.astype(BF16)) / safe
-            level = jnp.where(some, largest + jnp.log(safe), masked)
+            level = jnp.where(some, largest + jnp.log2(safe), masked)
             first = level.astype(BF16)
             rest = level - first.astype(F32)
             second = rest.astype(BF16)
@@ -117,40 +140,58 @@
         top = levels[0]
         for level in levels[1:]:
             top = jnp.maximum(top, level)
-        shares = [jnp.exp(level - top) for level in levels]
+        shares = [jnp.exp2(level - top) for level in levels]
         rows = slice(h * VDIM, (h + 1) * VDIM)
         whole = sum(shares)
         added = sum(parts[s, rows, :].astype(F32) * shares[s] for s in range(count))
         out[rows, :] = (added / whole).astype(BF16)
 
 
-def project_body(w, mine, theirs, place, out):
-    total = 0.0
+def project_body(w, mine, theirs, place, out, total):
+    step = pl.program_id(0)
     rows = w.shape[0] * w.shape[2]
-    for g in range(4):
-        group = place[0] ^ g
+    added = 0.0
+    for g in range(w.shape[1]):
+        group = place[0] ^ (step * w.shape[1] + g)
         tokens = jnp.concatenate([mine[group], theirs[group]], axis=1)
-        total = total + dot(w[:, g].reshape(rows, w.shape[3]), tokens)
-    out[...] = total.astype(BF16).reshape(out.shape)
+        added = added + dot(w[:, g].reshape(rows, w.shape[3]), tokens)
+
+    @pl.when(step == 0)
+    def _():
+        total[...] = added
+
+    @pl.when(step > 0)
+    def _():
+        total[...] += added
+
+    @pl.when(step == pl.num_programs(0) - 1)
+    def _():
+        here = place[1]
+        tile = w.shape[2]
+        for z in range(w.shape[0]):
+            piece = total[z * tile : (z + 1) * tile, :].astype(BF16)
+            out[z % 4, here, z // 4] = piece[:, :TOK]
+            out[z % 4, 1 - here, z // 4] = piece[:, TOK:]
 
 
 def project(w, mine, theirs, place):
-    tiles, _, rows, depth = w.shape
+    tiles, groups, rows, depth = w.shape
     wide = 2 * TOK
     return pl.pallas_call(
         project_body,
-        grid=(tiles // 2,),
-        out_shape=jax.ShapeDtypeStruct((tiles, rows, wide), BF16),
+        grid=(groups // 2,),
+        out_shape=jax.ShapeDtypeStruct((tiles // 2, 2, 2, rows, TOK), BF16),
         in_specs=[
-            pl.BlockSpec((2, 4, rows, depth), lambda i: (i, 0, 0, 0)),
+            pl.BlockSpec((tiles, 2, rows, depth), lambda i: (0, i, 0, 0)),
             pl.BlockSpec(mine.shape, lambda i: (0, 0, 0)),
             pl.BlockSpec(mine.shape, lambda i: (0, 0, 0)),
             pl.BlockSpec(memory_space=pltpu.SMEM),
         ],
-        out_specs=pl.BlockSpec((2, rows, wide), lambda i: (i, 0, 0)),
+        out_specs=pl.BlockSpec((tiles // 2, 2, 2, rows, TOK), lambda i: (0, 0, 0, 0, 0)),
+        scratch_shapes=[pltpu.VMEM((tiles * rows, wide), F32)],
         compiler_params=pltpu.CompilerParams(vmem_limit_bytes=LIMIT),
         cost_estimate=pl.CostEstimate(
-            flops=8 * tiles * rows * depth * wide, bytes_accessed=5_000_000, transcendentals=0
+            flops=2 * groups * tiles * rows * depth * wide, bytes_accessed=5_000_000, transcendentals=0
         ),
     )(w, mine, theirs, place)
 
@@ -168,23 +209,17 @@
 
 
 def shards(q_latent, latent_cache, w_q_up, w_kv_up, w_out, token_pos, start_offset):
-    pos_rows = jnp.concatenate(
-        [(token_pos >> 6)[None], (token_pos & 63)[None], jnp.zeros((14, TOK), jnp.int32)], axis=0
-    ).astype(BF16)
-
     columns = w_out.T.reshape(2, -1, HEADS * VDIM)
     xh = lax.axis_index("xh")
     halves = [lax.dynamic_index_in_dim(columns, xh ^ half, 0, keepdims=False) for half in range(2)]
     w_mine = [
         lax.ppermute(halves[half], ("xl", "xh", "yl"), crossed(half, flip))
+        for flip in range(2)
         for half in range(2)
-        for flip in range(2)
     ]
-    keys = jnp.concatenate([latent_cache.T, pos_rows], axis=0)
+    keys = kernel_call(pack_body, (KROWS, TOK), (latent_cache.T, token_pos[None]))
     keys = lax.all_gather(keys, ("za", "zb"), axis=0, tiled=False)
     latent = sent_to_all(q_latent.T, ("xh", "yh", "yl")).reshape(QL, TOK)
-    latent, w_mine = lax.optimization_barrier((latent, w_mine))
-    w_all = lax.all_gather(jnp.stack(w_mine), ("za", "zb"), axis=0, tiled=False)
 
     absolute = (token_pos + start_offset[0]).astype(F32)
     freqs = rope_base ** (-jnp.arange(ROPE // 2, dtype=F32) * 2.0 / ROPE)
@@ -192,14 +227,14 @@
     query = kernel_call(
         query_body,
         (QROWS, TOK),
-        (latent, w_q_up.T, jnp.cos(angle), jnp.sin(angle), pos_rows),
+        (latent, w_q_up, jnp.cos(angle), jnp.sin(angle), token_pos[None]),
         flops=300_000_000,
     )
+    query, w_mine = lax.optimization_barrier((query, w_mine))
+    w_all = lax.all_gather(jnp.stack(w_mine), ("za", "zb"), axis=0, tiled=False)
     queries = lax.all_gather(query, NEAR, axis=0, tiled=False)
 
-    per_head = w_kv_up.reshape(KVL, HEADS, NOPE + VDIM)
-    w_key = per_head[:, :, :NOPE].reshape(KVL, HEADS * NOPE)
-    w_value_t = per_head[:, :, NOPE:].reshape(KVL, HEADS * VDIM).T
+    w_key, w_value_t = kernel_call(weights_body, [(KVL, HEADS * NOPE), (HEADS * VDIM, KVL)], (w_kv_up,))
     count = keys.shape[0] * TOK
     parts = kernel_call(
         attend_body,
@@ -216,17 +251,14 @@
     )
     parts = lax.all_to_all(parts, NEAR, split_axis=0, concat_axis=0, tiled=True)
     mine = kernel_call(merge_body, (HEADS * VDIM, TOK), (parts,), flops=1_000_000)
-    mine = lax.all_gather(mine, ("xh", "yl"), axis=0, tiled=False)
+    mine = sent_to_all(mine, ("yl", "xh"))
     theirs = lax.ppermute(mine, "core", [(0, 1), (1, 0)])
-    place = (xh * 2 + lax.axis_index("xl")).astype(jnp.int32)[None]
+    place = jnp.stack([lax.axis_index("xl") * 2 + xh, lax.axis_index("core")]).astype(jnp.int32)
     partial = project(w_all, mine, theirs, place)
-    arrived = lax.all_to_all(partial, ("xh", "yh"), split_axis=0, concat_axis=0, tiled=True)
-    arrived = arrived.reshape(2, 4, -1, 2 * TOK)
-    summed = arrived.astype(F32).sum(axis=1).astype(BF16).reshape(-1, 2 * TOK)
-    kept = summed[:, :TOK]
-    got = lax.ppermute(summed[:, TOK:], "core", [(0, 1), (1, 0)])
-    first = lax.axis_index("core") == 0
-    return jnp.concatenate([jnp.where(first, kept, got), jnp.where(first, got, kept)], axis=0).T
+    partial = partial.reshape(16, -1, TOK)
+    arrived = lax.all_to_all(partial, ("yh", "core", "xh"), split_axis=0, concat_axis=0, tiled=True)
+    arrived = arrived.reshape(4, 4, -1, TOK)
+    return arrived.astype(F32).sum(axis=0).astype(BF16).reshape(-1, TOK).T
 
 
 def solution(mesh):

time: 154 us -> 151 us (0.981)
  blocking collectives: 59.8 us -> 66.1 us
  starting transfers between devices: 33.2 us -> 27.3 us
  local copies, waits for them, and re-layouts: 10.1 us -> 4.26 us
  Pallas kernels: 20 us -> 23.1 us
  other arithmetic: 5.32 us -> 3.57 us
    all_to_all x1 -> x2, blocking collectives: 23.6 us -> 40.9 us  [the longest x1 27.5 us: shards(): lax.all_to_all(partial, ('yh', 'core', 'xh'), split_axis=0, concat_axis=0...]
    all_gather x1 -> x0, blocking collectives: 13.7 us -> none  [shards(): mine = lax.all_gather(mine, ('xh', 'yl'), axis=0, tiled=False)]
    all_gather x1, waiting for transfers between devices: 0.01 us -> 8.09 us  [shards(): w_all = lax.all_gather(jnp.stack(w_mine), ('za', 'zb'), axis=0, tiled=False)]
    ppermute x4, waiting for transfers between devices: 8.46 us -> 2.54 us  [shards(): lax.ppermute(halves[half], ('xl', 'xh', 'yl'), crossed(half, flip))]
    unnamed x11 -> x8, local copies, waits for them, and re-layouts: 5.32 us -> 0.77 us
    ppermute x1 -> x0, starting transfers between devices: 4.1 us -> none  [shards(): got = lax.ppermute(summed[:, TOK:], 'core', [(0, 1), (1, 0)])]
    pallas_call x4 -> x6, Pallas kernels: 20 us -> 23.1 us  [the longest x5 19 us: kernel_call(): pl.pallas_call(body, out_shape=outs[0] if single else outs, in_specs=spec...]
    all_to_all x1, blocking collectives: 13 us -> 16 us  [shards(): parts = lax.all_to_all(parts, NEAR, split_axis=0, concat_axis=0, tiled=True)]
  transfers between devices with their start and end apart: 9 -> 8, of which waited for: 5 -> 3; matrix products, arithmetic and copies ran while one was open for 8% -> 4% of each run, Pallas kernels for 10% -> 12%
where the time goes in v3:
time: 151 us; the launch traced here: 150 us
  blocking collectives  66.1 us (44%)
  starting transfers between devices  27.3 us (18%)
  Pallas kernels  23.1 us (15%)
  between operations  14.2 us (9%)
  waiting for transfers between devices  11.6 us (8%)
  local copies, waits for them, and re-layouts  4.26 us (3%)
  other arithmetic  3.57 us (2%)
    all_to_all x1, blocking collectives, shards(): lax.all_to_all(partial, ('yh', 'core', 'xh'), split_axis=0, concat_axis=0...  27.5 us
    pallas_call x5, Pallas kernels, kernel_call(): pl.pallas_call(body, out_shape=outs[0] if single else outs, in_specs=spec...  19 us
    all_to_all x1, blocking collectives, shards(): parts = lax.all_to_all(parts, NEAR, split_axis=0, concat_axis=0, tiled=True)  16 us
    all_to_all x1, blocking collectives, sent_to_all(): return lax.all_to_all(copies, axis, split_axis=0, concat_axis=0, tiled=True)  13.4 us
    ppermute x4, starting transfers between devices, shards(): lax.ppermute(halves[half], ('xl', 'xh', 'yl'), crossed(half, flip))  12.9 us
    all_to_all x1, starting transfers between devices, sent_to_all(): return lax.all_to_all(copies, axis, split_axis=0, concat_axis=0, tiled=True)  10.2 us
    all_gather x1, blocking collectives, shards(): queries = lax.all_gather(query, NEAR, axis=0, tiled=False)  9.24 us
    all_gather x1, waiting for transfers between devices, shards(): w_all = lax.all_gather(jnp.stack(w_mine), ('za', 'zb'), axis=0, tiled=False)  8.09 us
  transfers between devices with their start and end apart: 8, of which 3 were waited for; matrix products, arithmetic and copies ran while one was open for 4% of the time, Pallas kernels for 12%

profile of v3, /device:TPU:1, one launch (start us, length us, event | category | flops | bytes accessed | tf_op | source)
XLA Modules:
  0.0 150.0 jit_solution(914890477995805455)
XLA Ops:
  6.5 0.0 all-gather.8.cloned.1.call-start
  6.5 1.6 %shard_map.74 = bf16[592,128]{1,0:T(8,128)(2,1)} custom-call(bf16[576,128]{1,0:T(8,128)(2,1)} %bitcast.33, s32[1,128]{1,0:T(1,128)} %bitcast.39), custom_call_target="tpu_custom_call" | custom-call | bytes 4000000 | tf_op jit(solution)/shard_map/pallas_call | solution.py:44
  8.1 0.0 all-gather.8.cloned.1.call-update
  8.2 1.5 %broadcast_in_dim.12 = bf16[16,96,128]{2,1,0:T(8,128)(2,1)} broadcast(bf16[96,128]{1,0:T(8,128)(2,1)} %bitcast.38), dimensions={1,2} | broadcast | bytes 417792 | tf_op jit(solution)/shard_map/broadcast_in_dim | solution.py:200
  9.7 10.2 %all-to-all-start = ((bf16[16,96,128]{2,1,0:T(8,128)(2,1)}), bf16[16,96,128]{2,1,0:T(8,128)(2,1)S(1)}, u32[]{:S(2)}, u32[]{:S(2)}) async-start(bf16[16,96,128]{2,1,0:T(8,128)(2,1)} %broadcast_in_dim.12), calls=%async_computation | async-start | bytes 786432 | tf_op jit(solution)/shard_map/all_to_all | solution.py:201
  19.9 0.0 all-gather.6.cloned.1.call-start
  20.0 1.0 dynamic-slice_bitcast_fusion
  21.0 0.7 collective-permute-start
  21.6 5.7 %collective-permute-start.2 = (bf16[112,512]{1,0:T(8,128)(2,1)S(1)}, bf16[112,512]{1,0:T(8,128)(2,1)S(1)}, u32[]{:S(2)}, u32[]{:S(2)}) collective-permute-start(bf16[112,512]{1,0:T(8,128)(2,1)S(1)} %get-tuple-element.20), channel_id=1, source_target_pairs={{0,32},{1,0},{8,40},{9,8},{32,33},{33,1},{40,41},{41,9},{2,34},{3,... | collective-permute-start | bytes 344072 | tf_op jit(solution)/shard_map/ppermute | solution.py:216
  27.3 4.6 %collective-permute-start.1 = (bf16[112,512]{1,0:T(8,128)(2,1)S(1)}, bf16[112,512]{1,0:T(8,128)(2,1)S(1)}, u32[]{:S(2)}, u32[]{:S(2)}) collective-permute-start(bf16[112,512]{1,0:T(8,128)(2,1)S(1)} %get-tuple-element.19), channel_id=1, source_target_pairs={{0,8},{1,40},{8,0},{9,32},{32,9},{33,41},{40,1},{41,33},{2,10},{3,... | collective-permute-start | bytes 344072 | tf_op jit(solution)/shard_map/ppermute | solution.py:216
  31.9 1.9 %collective-permute-start.3 = (bf16[112,512]{1,0:T(8,128)(2,1)S(1)}, bf16[112,512]{1,0:T(8,128)(2,1)S(1)}, u32[]{:S(2)}, u32[]{:S(2)}) collective-permute-start(bf16[112,512]{1,0:T(8,128)(2,1)S(1)} %get-tuple-element.19), channel_id=1, source_target_pairs={{0,40},{1,8},{8,32},{9,0},{32,41},{33,9},{40,33},{41,1},{2,42},{3,... | collective-permute-start | bytes 344072 | tf_op jit(solution)/shard_map/ppermute | solution.py:216
  34.5 0.7 add_convert_fusion
  35.2 0.8 multiply_sine_fusion
  35.9 0.0 all-to-all-done
  36.0 0.0 copy-start.1
  36.0 0.8 copy-done.1
  36.7 3.1 %shard_map.73 = bf16[784,128]{1,0:T(8,128)(2,1)} custom-call(bf16[1536,128]{1,0:T(8,128)(2,1)} %bitcast.30, bf16[1536,768]{1,0:T(8,128)(2,1)} %weights.1, f32[32,128]{1,0:T(8,128)} %get-tuple-element.22.cosine, f32[32,128]{1,0:T(8,128)} %get-tuple-element.21.sine, s32[1,128]{1,0:T(1,128)} %bitcast.40), custom_call_target="tpu_custom_call" | custom-call | flops 300000000 | bytes 4000000 | tf_op jit(solution)/shard_map/pallas_call | solution.py:44
  39.8 0.0 copy-start.2
  39.8 0.0 collective-permute-done
  39.8 0.0 collective-permute-done.1
  39.8 0.0 collective-permute-done.2
  39.8 2.5 %collective-permute-done.3 = bf16[112,512]{1,0:T(8,128)(2,1)S(1)} collective-permute-done((bf16[112,512]{1,0:T(8,128)(2,1)S(1)}, bf16[112,512]{1,0:T(8,128)(2,1)S(1)}, u32[]{:S(2)}, u32[]{:S(2)}) %collective-permute-start.3) | collective-permute-done | bytes 114720 | tf_op jit(solution)/shard_map/ppermute | solution.py:216
  42.3 0.8 pad_maximum_fusion
  43.2 0.0 all-gather.6.cloned.1.call-update
  43.2 2.4 %shard_map.75 = (bf16[512,512]{1,0:T(8,128)(2,1)}, bf16[512,512]{1,0:T(8,128)(2,1)}) custom-call(bf16[512,1024]{1,0:T(8,128)(2,1)} %w.1), custom_call_target="tpu_custom_call" | custom-call | bytes 4000000 | tf_op jit(solution)/shard_map/pallas_call | solution.py:44
  45.6 0.0 copy-done.2
  45.6 9.2 %all-gather.1 = bf16[3136,128]{1,0:T(8,128)(2,1)} all-gather(bf16[784,128]{1,0:T(8,128)(2,1)S(1)} %copy-done.2), channel_id=3, replica_groups=mesh['za'=2,'zb'=4,'xl'=2,'core'=2,'xh'=2,'yh'=4,'yl'=2] {'xl','core'}, dimensions={0}, use_global_device_ids=true | all-gather | bytes 1003520 | tf_op jit(solution)/shard_map/all_gather | solution.py:235
  54.9 0.0 all-gather.8.cloned.1.call-done
  54.9 10.1 %shard_map.76 = bf16[4,528,128]{2,1,0:T(8,128)(2,1)} custom-call(bf16[4,784,128]{2,1,0:T(8,128)(2,1)} %bitcast.31, bf16[8,592,128]{2,1,0:T(8,128)(2,1)} %bitcast.41, bf16[512,512]{1,0:T(8,128)(2,1)} %get-tuple-element.17.w_key, bf16[512,512]{1,0:T(8,128)(2,1)} %get-tuple-element.18.w_value_t), custom_call_target="tpu_custom_call" | custom-call | flops 3500000000 | bytes 4000000 | tf_op jit(solution)/shard_map/pallas_call | solution.py:44
  64.9 16.0 %all_to_all.20.parts = bf16[4,528,128]{2,1,0:T(8,128)(2,1)} all-to-all(bf16[4,528,128]{2,1,0:T(8,128)(2,1)} %shard_map.76), channel_id=1, replica_groups=mesh['za'=2,'zb'=4,'xl'=2,'core'=2,'xh'=2,'yh'=4,'yl'=2] {'xl','core'}, dimensions={0} | all-to-all | bytes 1081344 | tf_op jit(solution)/shard_map/all_to_all | solution.py:252
  80.9 1.9 %shard_map.77 = bf16[512,128]{1,0:T(8,128)(2,1)} custom-call(bf16[4,528,128]{2,1,0:T(8,128)(2,1)} %all_to_all.20.parts), custom_call_target="tpu_custom_call" | custom-call | flops 1000000 | bytes 4000000 | tf_op jit(solution)/shard_map/pallas_call | solution.py:44
  82.8 1.0 broadcast_in_dim.14
  83.8 13.4 %all_to_all.21.mine = bf16[4,512,128]{2,1,0:T(8,128)(2,1)S(1)} all-to-all(bf16[4,512,128]{2,1,0:T(8,128)(2,1)S(1)} %broadcast_in_dim.14), channel_id=1, replica_groups=mesh['za'=2,'zb'=4,'xl'=2,'core'=2,'xh'=2,'yh'=4,'yl'=2] {'yl','xh'}, dimensions={0} | all-to-all | bytes 1048576 | tf_op jit(solution)/shard_map/all_to_all | solution.py:201
  97.2 0.0 copy-start
  97.2 4.1 %collective-permute-start.4 = (bf16[4,512,128]{2,1,0:T(8,128)(2,1)S(1)}, bf16[4,512,128]{2,1,0:T(8,128)(2,1)S(1)}, u32[]{:S(2)}, u32[]{:S(2)}) collective-permute-start(bf16[4,512,128]{2,1,0:T(8,128)(2,1)S(1)} %all_to_all.21.mine), channel_id=1, source_target_pairs={{0,16},{16,0},{1,17},{17,1},{2,18},{18,2},{3,19},{19,3},{4,20},{20... | collective-permute-start | bytes 1572872 | tf_op jit(solution)/shard_map/ppermute | solution.py:255
  101.3 0.6 pad_add_fusion.place
  102.0 0.9 collective-permute-done.4.theirs
  102.9 0.0 copy-start.3
  102.9 8.1 %all-gather.6.cloned.1.call-done = bf16[32,112,512]{2,1,0:T(8,128)(2,1)} async-done(((bf16[4,112,512]{2,1,0:T(8,128)(2,1)}), bf16[32,112,512]{2,1,0:T(8,128)(2,1)}) %all-gather.6.cloned.1.call-update) | async-done | bytes 3670032 | tf_op jit(solution)/shard_map/all_gather | solution.py:234
  110.9 0.0 copy-done
  110.9 0.0 copy-done.3
  110.9 4.1 %shard_map.78 = bf16[4,2,2,112,128]{4,3,2,1,0:T(8,128)(2,1)} custom-call(bf16[8,4,112,512]{3,2,1,0:T(8,128)(2,1)} %bitcast.27, bf16[4,512,128]{2,1,0:T(8,128)(2,1)} %copy-done, bf16[4,512,128]{2,1,0:T(8,128)(2,1)} %copy-done.3, s32[2]{0:T(128)} %pad_add_fusion.place), custom_call_target="tpu_custom_call" | custom-call | flops 939524096 | bytes 5000000 | tf_op jit(solution)/shard_map/pallas_call | solution.py:180
  115.0 27.5 %all_to_all.22 = bf16[16,112,128]{2,1,0:T(8,128)(2,1)S(1)} all-to-all(bf16[16,112,128]{2,1,0:T(8,128)(2,1)} %bitcast.29), channel_id=1, replica_groups=mesh['za'=2,'zb'=4,'xl'=2,'core'=2,'xh'=2,'yh'=4,'yl'=2] {'yh','core','xh'}, dimensions={0} | all-to-all | bytes 917504 | tf_op jit(solution)/shard_map/all_to_all | solution.py:259
  142.5 0.7 reduce_sum.12
  (1 shorter events, 0.0 us)
Async XLA Ops:
  6.5 48.3 %all-gather.8.cloned.1.call-start = ((), (), s32[]{:S(2)}) async-start(), calls=%async_computation.5 | async-start | bytes 1363968 | tf_op jit(solution)/shard_map/all_gather | solution.py:221
  9.7 26.2 %all-to-all-start = ((bf16[16,96,128]{2,1,0:T(8,128)(2,1)}), bf16[16,96,128]{2,1,0:T(8,128)(2,1)S(1)}, u32[]{:S(2)}, u32[]{:S(2)}) async-start(bf16[16,96,128]{2,1,0:T(8,128)(2,1)} %broadcast_in_dim.12), calls=%async_computation | async-start | bytes 786432 | tf_op jit(solution)/shard_map/all_to_all | solution.py:201
  19.9 91.0 %all-gather.6.cloned.1.call-start = ((), (), s32[]{:S(2)}) async-start(), calls=%async_computation.4 | async-start | bytes 4128768 | tf_op jit(solution)/shard_map/all_gather | solution.py:234
  21.0 18.8 %collective-permute-start = (bf16[112,512]{1,0:T(8,128)(2,1)S(1)}, bf16[112,512]{1,0:T(8,128)(2,1)S(1)}, u32[]{:S(2)}, u32[]{:S(2)}) collective-permute-start(bf16[112,512]{1,0:T(8,128)(2,1)S(1)} %get-tuple-element.20), channel_id=1, source_target_pairs={{0,0},{1,32},{8,8},{9,40},{32,1},{33,33},{40,9},{41,41},{2,2},{3,3... | collective-permute-start | bytes 344072 | tf_op jit(solution)/shard_map/ppermute | solution.py:216
  21.6 18.2 %collective-permute-start.2 = (bf16[112,512]{1,0:T(8,128)(2,1)S(1)}, bf16[112,512]{1,0:T(8,128)(2,1)S(1)}, u32[]{:S(2)}, u32[]{:S(2)}) collective-permute-start(bf16[112,512]{1,0:T(8,128)(2,1)S(1)} %get-tuple-element.20), channel_id=1, source_target_pairs={{0,32},{1,0},{8,40},{9,8},{32,33},{33,1},{40,41},{41,9},{2,34},{3,... | collective-permute-start | bytes 344072 | tf_op jit(solution)/shard_map/ppermute | solution.py:216
  27.3 12.5 %collective-permute-start.1 = (bf16[112,512]{1,0:T(8,128)(2,1)S(1)}, bf16[112,512]{1,0:T(8,128)(2,1)S(1)}, u32[]{:S(2)}, u32[]{:S(2)}) collective-permute-start(bf16[112,512]{1,0:T(8,128)(2,1)S(1)} %get-tuple-element.19), channel_id=1, source_target_pairs={{0,8},{1,40},{8,0},{9,32},{32,9},{33,41},{40,1},{41,33},{2,10},{3,... | collective-permute-start | bytes 344072 | tf_op jit(solution)/shard_map/ppermute | solution.py:216
  31.9 10.4 %collective-permute-start.3 = (bf16[112,512]{1,0:T(8,128)(2,1)S(1)}, bf16[112,512]{1,0:T(8,128)(2,1)S(1)}, u32[]{:S(2)}, u32[]{:S(2)}) collective-permute-start(bf16[112,512]{1,0:T(8,128)(2,1)S(1)} %get-tuple-element.19), channel_id=1, source_target_pairs={{0,40},{1,8},{8,32},{9,0},{32,41},{33,9},{40,33},{41,1},{2,42},{3,... | collective-permute-start | bytes 344072 | tf_op jit(solution)/shard_map/ppermute | solution.py:216
  36.0 0.8 copy-start.1
  39.8 5.8 %copy-start.2 = (bf16[784,128]{1,0:T(8,128)(2,1)S(1)}, bf16[784,128]{1,0:T(8,128)(2,1)}, u32[]{:S(2)}) copy-start(bf16[784,128]{1,0:T(8,128)(2,1)} %shard_map.73) | copy-start | bytes 602116
  97.2 13.8 %copy-start = (bf16[4,512,128]{2,1,0:T(8,128)(2,1)}, bf16[4,512,128]{2,1,0:T(8,128)(2,1)S(1)}, u32[]{:S(2)}) copy-start(bf16[4,512,128]{2,1,0:T(8,128)(2,1)S(1)} %all_to_all.21.mine) | copy-start | bytes 1572868
  97.2 5.7 %collective-permute-start.4 = (bf16[4,512,128]{2,1,0:T(8,128)(2,1)S(1)}, bf16[4,512,128]{2,1,0:T(8,128)(2,1)S(1)}, u32[]{:S(2)}, u32[]{:S(2)}) collective-permute-start(bf16[4,512,128]{2,1,0:T(8,128)(2,1)S(1)} %all_to_all.21.mine), channel_id=1, source_target_pairs={{0,16},{16,0},{1,17},{17,1},{2,18},{18,2},{3,19},{19,3},{4,20},{20... | collective-permute-start | bytes 1572872 | tf_op jit(solution)/shard_map/ppermute | solution.py:255
  102.9 8.1 %copy-start.3 = (bf16[4,512,128]{2,1,0:T(8,128)(2,1)}, bf16[4,512,128]{2,1,0:T(8,128)(2,1)S(1)}, u32[]{:S(2)}) copy-start(bf16[4,512,128]{2,1,0:T(8,128)(2,1)S(1)} %collective-permute-done.4.theirs) | copy-start | bytes 1572868
Sparse Core Ops, SparseCore 0:
  9.4 44.1 all-gather.7
  55.7 55.1 all-gather.5

commit v4 on v3

--- a/solution.py
+++ b/solution.py
@@ -153,7 +153,7 @@
     added = 0.0
     for g in range(w.shape[1]):
         group = place[0] ^ (step * w.shape[1] + g)
-        tokens = jnp.concatenate([mine[group], theirs[group]], axis=1)
+        tokens = jnp.concatenate([x[2 * group + t] for x in (mine, theirs) for t in range(2)], axis=1)
         added = added + dot(w[:, g].reshape(rows, w.shape[3]), tokens)
 
     @pl.when(step == 0)
@@ -170,24 +170,26 @@
         tile = w.shape[2]
         for z in range(w.shape[0]):
             piece = total[z * tile : (z + 1) * tile, :].astype(BF16)
-            out[z % 4, here, z // 4] = piece[:, :TOK]
-            out[z % 4, 1 - here, z // 4] = piece[:, TOK:]
+            for t in range(2):
+                near, far = t * TOK, (t + 2) * TOK
+                out[z % 4, here, z // 4, t] = piece[:, near : near + TOK]
+                out[z % 4, 1 - here, z // 4, t] = piece[:, far : far + TOK]
 
 
 def project(w, mine, theirs, place):
     tiles, groups, rows, depth = w.shape
-    wide = 2 * TOK
+    wide = 4 * TOK
     return pl.pallas_call(
         project_body,
         grid=(groups // 2,),
-        out_shape=jax.ShapeDtypeStruct((tiles // 2, 2, 2, rows, TOK), BF16),
+        out_shape=jax.ShapeDtypeStruct((tiles // 2, 2, 2, 2, rows, TOK), BF16),
         in_specs=[
             pl.BlockSpec((tiles, 2, rows, depth), lambda i: (0, i, 0, 0)),
             pl.BlockSpec(mine.shape, lambda i: (0, 0, 0)),
             pl.BlockSpec(mine.shape, lambda i: (0, 0, 0)),
             pl.BlockSpec(memory_space=pltpu.SMEM),
         ],
-        out_specs=pl.BlockSpec((tiles // 2, 2, 2, rows, TOK), lambda i: (0, 0, 0, 0, 0)),
+        out_specs=pl.BlockSpec((tiles // 2, 2, 2, 2, rows, TOK), lambda i: (0, 0, 0, 0, 0, 0)),
         scratch_shapes=[pltpu.VMEM((tiles * rows, wide), F32)],
         compiler_params=pltpu.CompilerParams(vmem_limit_bytes=LIMIT),
         cost_estimate=pl.CostEstimate(
@@ -209,11 +211,16 @@
 
 
 def shards(q_latent, latent_cache, w_q_up, w_kv_up, w_out, token_pos, start_offset):
-    columns = w_out.T.reshape(2, -1, HEADS * VDIM)
+    columns = w_out.T.reshape(4, -1, HEADS * VDIM)
+    part = columns.shape[1]
+    yl = lax.axis_index("yl")
     xh = lax.axis_index("xh")
-    halves = [lax.dynamic_index_in_dim(columns, xh ^ half, 0, keepdims=False) for half in range(2)]
     w_mine = [
-        lax.ppermute(halves[half], ("xl", "xh", "yl"), crossed(half, flip))
+        lax.ppermute(
+            lax.dynamic_index_in_dim(columns, (xh ^ half) * 2 + (yl ^ flip), 0, keepdims=False),
+            ("xl", "xh", "yl"),
+            crossed(half, flip),
+        )
         for flip in range(2)
         for half in range(2)
     ]
@@ -231,7 +238,8 @@
         flops=300_000_000,
     )
     query, w_mine = lax.optimization_barrier((query, w_mine))
-    w_all = lax.all_gather(jnp.stack(w_mine), ("za", "zb"), axis=0, tiled=False)
+    w_four = jnp.pad(jnp.stack(w_mine), ((0, 0), (0, -part % 16), (0, 0)))
+    w_all = lax.all_gather(w_four, ("za", "zb"), axis=0, tiled=False)
     queries = lax.all_gather(query, NEAR, axis=0, tiled=False)
 
     w_key, w_value_t = kernel_call(weights_body, [(KVL, HEADS * NOPE), (HEADS * VDIM, KVL)], (w_kv_up,))
@@ -251,13 +259,13 @@
     )
     parts = lax.all_to_all(parts, NEAR, split_axis=0, concat_axis=0, tiled=True)
     mine = kernel_call(merge_body, (HEADS * VDIM, TOK), (parts,), flops=1_000_000)
-    mine = sent_to_all(mine, ("yl", "xh"))
+    mine = sent_to_all(mine, ("yl", "xh", "xl"))
     theirs = lax.ppermute(mine, "core", [(0, 1), (1, 0)])
     place = jnp.stack([lax.axis_index("xl") * 2 + xh, lax.axis_index("core")]).astype(jnp.int32)
     partial = project(w_all, mine, theirs, place)
-    partial = partial.reshape(16, -1, TOK)
-    arrived = lax.all_to_all(partial, ("yh", "core", "xh"), split_axis=0, concat_axis=0, tiled=True)
-    arrived = arrived.reshape(4, 4, -1, TOK)
+    partial = partial.reshape(32, -1, TOK)
+    arrived = lax.all_to_all(partial, ("yh", "core", "xh", "xl"), split_axis=0, concat_axis=0, tiled=True)
+    arrived = arrived.reshape(4, 8, -1, TOK)[:, :, :part]
     return arrived.astype(F32).sum(axis=0).astype(BF16).reshape(-1, TOK).T
 
 

time: 151 us -> 147 us (0.974)
  waiting for transfers between devices: 11.6 us -> 1.72 us
  blocking collectives: 66.1 us -> 71.5 us
    all_gather x1, waiting for transfers between devices: 8.09 us -> 0.01 us  [shards(): w_all = lax.all_gather(w_four, ('za', 'zb'), axis=0, tiled=False)]
    all_to_all x1, blocking collectives: 13.4 us -> 19.1 us  [sent_to_all(): return lax.all_to_all(copies, axis, split_axis=0, concat_axis=0, tiled=True)]
    all_to_all x1, blocking collectives: 27.5 us -> 23.1 us  [shards(): lax.all_to_all(partial, ('yh', 'core', 'xh', 'xl'), split_axis=0, concat_...]
    all_gather x1, blocking collectives: 9.24 us -> 12 us  [shards(): queries = lax.all_gather(query, NEAR, axis=0, tiled=False)]
    ppermute x4, waiting for transfers between devices: 2.54 us -> 0.01 us  [shards(): lax.ppermute(lax.dynamic_index_in_dim(columns, (xh ^ half) * 2 + (yl ^ fl...]
  transfers between devices with their start and end apart: 8 -> 8, of which waited for: 3 -> 1; matrix products, arithmetic and copies ran while one was open for 4% -> 4% of each run, Pallas kernels for 12% -> 12%
where the time goes in v4:
time: 147 us; the launch traced here: 145 us
  blocking collectives  71.5 us (49%)
  starting transfers between devices  26.5 us (18%)
  Pallas kernels  23.3 us (16%)
  between operations  14.2 us (10%)
  local copies, waits for them, and re-layouts  5.26 us (4%)
  other arithmetic  2.8 us (2%)
  waiting for transfers between devices  1.72 us (1%)
    all_to_all x1, blocking collectives, shards(): lax.all_to_all(partial, ('yh', 'core', 'xh', 'xl'), split_axis=0, concat_...  23.1 us
    all_to_all x1, blocking collectives, sent_to_all(): return lax.all_to_all(copies, axis, split_axis=0, concat_axis=0, tiled=True)  19.1 us
    pallas_call x5, Pallas kernels, kernel_call(): pl.pallas_call(body, out_shape=outs[0] if single else outs, in_specs=spec...  19 us
    all_to_all x1, blocking collectives, shards(): parts = lax.all_to_all(parts, NEAR, split_axis=0, concat_axis=0, tiled=True)  17.3 us
    all_gather x1, blocking collectives, shards(): queries = lax.all_gather(query, NEAR, axis=0, tiled=False)  12 us
    ppermute x4, starting transfers between devices, shards(): lax.ppermute(lax.dynamic_index_in_dim(columns, (xh ^ half) * 2 + (yl ^ fl...  12 us
    all_to_all x1, starting transfers between devices, sent_to_all(): return lax.all_to_all(copies, axis, split_axis=0, concat_axis=0, tiled=True)  10.2 us
    pallas_call x1, Pallas kernels, project(): pl.pallas_call(project_body, grid=(groups // 2,), out_shape=jax.ShapeDtyp...  4.32 us
  transfers between devices with their start and end apart: 8, of which 1 were waited for; matrix products, arithmetic and copies ran while one was open for 4% of the time, Pallas kernels for 12%

profile of v4, /device:TPU:1, one launch (start us, length us, event | category | flops | bytes accessed | tf_op | source)
XLA Modules:
  0.0 145.3 jit_solution(12354987239117754295)
XLA Ops:
  6.5 0.0 copy-start.3
  6.5 0.0 all-gather.8.cloned.1.call-start
  6.5 1.6 %shard_map.74 = bf16[592,128]{1,0:T(8,128)(2,1)} custom-call(bf16[576,128]{1,0:T(8,128)(2,1)} %bitcast.37, s32[1,128]{1,0:T(1,128)} %bitcast.43), custom_call_target="tpu_custom_call" | custom-call | bytes 4000000 | tf_op jit(solution)/shard_map/pallas_call | solution.py:44
  8.1 0.0 all-gather.8.cloned.1.call-update
  8.2 1.5 %broadcast_in_dim.12 = bf16[16,96,128]{2,1,0:T(8,128)(2,1)} broadcast(bf16[96,128]{1,0:T(8,128)(2,1)} %bitcast.42), dimensions={1,2} | broadcast | bytes 417792 | tf_op jit(solution)/shard_map/broadcast_in_dim | solution.py:202
  9.7 10.2 %all-to-all-start = ((bf16[16,96,128]{2,1,0:T(8,128)(2,1)}), bf16[16,96,128]{2,1,0:T(8,128)(2,1)S(1)}, u32[]{:S(2)}, u32[]{:S(2)}) async-start(bf16[16,96,128]{2,1,0:T(8,128)(2,1)} %broadcast_in_dim.12), calls=%async_computation | async-start | bytes 786432 | tf_op jit(solution)/shard_map/all_to_all | solution.py:203
  19.9 0.0 all-gather.6.cloned.1.call-start
  20.0 0.9 dynamic-slice_bitcast_fusion
  20.9 0.7 collective-permute-start
  21.6 4.8 %collective-permute-start.1 = (bf16[56,512]{1,0:T(8,128)(2,1)S(1)}, bf16[56,512]{1,0:T(8,128)(2,1)S(1)}, u32[]{:S(2)}, u32[]{:S(2)}) collective-permute-start(bf16[56,512]{1,0:T(8,128)(2,1)S(1)} %get-tuple-element.21), channel_id=1, source_target_pairs={{0,8},{1,40},{8,0},{9,32},{32,9},{33,41},{40,1},{41,33},{2,10},{3,... | collective-permute-start | bytes 172040 | tf_op jit(solution)/shard_map/ppermute | solution.py:219
  26.4 4.6 %collective-permute-start.2 = (bf16[56,512]{1,0:T(8,128)(2,1)S(1)}, bf16[56,512]{1,0:T(8,128)(2,1)S(1)}, u32[]{:S(2)}, u32[]{:S(2)}) collective-permute-start(bf16[56,512]{1,0:T(8,128)(2,1)S(1)} %get-tuple-element.20), channel_id=1, source_target_pairs={{0,32},{1,0},{8,40},{9,8},{32,33},{33,1},{40,41},{41,9},{2,34},{3,... | collective-permute-start | bytes 172040 | tf_op jit(solution)/shard_map/ppermute | solution.py:219
  31.0 1.9 %collective-permute-start.3 = (bf16[56,512]{1,0:T(8,128)(2,1)S(1)}, bf16[56,512]{1,0:T(8,128)(2,1)S(1)}, u32[]{:S(2)}, u32[]{:S(2)}) collective-permute-start(bf16[56,512]{1,0:T(8,128)(2,1)S(1)} %get-tuple-element.19), channel_id=1, source_target_pairs={{0,40},{1,8},{8,32},{9,0},{32,41},{33,9},{40,33},{41,1},{2,42},{3,... | collective-permute-start | bytes 172040 | tf_op jit(solution)/shard_map/ppermute | solution.py:219
  33.6 0.0 copy-done.3
  33.6 0.8 multiply_sine_fusion
  34.4 2.4 %shard_map.75 = (bf16[512,512]{1,0:T(8,128)(2,1)}, bf16[512,512]{1,0:T(8,128)(2,1)}) custom-call(bf16[512,1024]{1,0:T(8,128)(2,1)} %w.1), custom_call_target="tpu_custom_call" | custom-call | bytes 4000000 | tf_op jit(solution)/shard_map/pallas_call | solution.py:44
  36.8 0.0 all-to-all-done
  36.8 0.0 copy-start.1
  36.8 0.7 copy-done.1
  37.6 3.1 %shard_map.73 = bf16[784,128]{1,0:T(8,128)(2,1)} custom-call(bf16[1536,128]{1,0:T(8,128)(2,1)} %bitcast.34, bf16[1536,768]{1,0:T(8,128)(2,1)} %weights.1, f32[32,128]{1,0:T(8,128)} %get-tuple-element.24.cosine, f32[32,128]{1,0:T(8,128)} %get-tuple-element.23.sine, s32[1,128]{1,0:T(1,128)} %bitcast.44), custom_call_target="tpu_custom_call" | custom-call | flops 300000000 | bytes 4000000 | tf_op jit(solution)/shard_map/pallas_call | solution.py:44
  40.7 0.0 collective-permute-done
  40.7 0.0 collective-permute-done.1
  40.7 0.0 collective-permute-done.2
  40.7 0.0 collective-permute-done.3
  40.7 0.7 fusion.6
  41.4 0.0 all-gather.6.cloned.1.call-update
  41.5 12.0 %all-gather.1 = bf16[3136,128]{1,0:T(8,128)(2,1)} all-gather(bf16[784,128]{1,0:T(8,128)(2,1)} %shard_map.73), channel_id=3, replica_groups=mesh['za'=2,'zb'=4,'xl'=2,'core'=2,'xh'=2,'yh'=4,'yl'=2] {'xl','core'}, dimensions={0}, use_global_device_ids=true | all-gather | bytes 1003520 | tf_op jit(solution)/shard_map/all_gather | solution.py:243
  53.5 0.0 all-gather.8.cloned.1.call-done
  53.5 10.1 %shard_map.76 = bf16[4,528,128]{2,1,0:T(8,128)(2,1)} custom-call(bf16[4,784,128]{2,1,0:T(8,128)(2,1)} %bitcast.35, bf16[8,592,128]{2,1,0:T(8,128)(2,1)} %bitcast.45, bf16[512,512]{1,0:T(8,128)(2,1)} %get-tuple-element.17.w_key, bf16[512,512]{1,0:T(8,128)(2,1)} %get-tuple-element.18.w_value_t), custom_call_target="tpu_custom_call" | custom-call | flops 3500000000 | bytes 4000000 | tf_op jit(solution)/shard_map/pallas_call | solution.py:44
  63.5 17.3 %all_to_all.20.parts = bf16[4,528,128]{2,1,0:T(8,128)(2,1)} all-to-all(bf16[4,528,128]{2,1,0:T(8,128)(2,1)} %shard_map.76), channel_id=1, replica_groups=mesh['za'=2,'zb'=4,'xl'=2,'core'=2,'xh'=2,'yh'=4,'yl'=2] {'xl','core'}, dimensions={0} | all-to-all | bytes 1081344 | tf_op jit(solution)/shard_map/all_to_all | solution.py:260
  80.8 1.8 %shard_map.77 = bf16[512,128]{1,0:T(8,128)(2,1)} custom-call(bf16[4,528,128]{2,1,0:T(8,128)(2,1)} %all_to_all.20.parts), custom_call_target="tpu_custom_call" | custom-call | flops 1000000 | bytes 4000000 | tf_op jit(solution)/shard_map/pallas_call | solution.py:44
  82.7 1.0 broadcast_in_dim.14
  83.7 19.1 %all_to_all.21.mine = bf16[8,512,128]{2,1,0:T(8,128)(2,1)S(1)} all-to-all(bf16[8,512,128]{2,1,0:T(8,128)(2,1)S(1)} %broadcast_in_dim.14), channel_id=1, replica_groups=mesh['za'=2,'zb'=4,'xl'=2,'core'=2,'xh'=2,'yh'=4,'yl'=2] {'yl','xh','xl'}, dimensions={0} | all-to-all | bytes 2097152 | tf_op jit(solution)/shard_map/all_to_all | solution.py:203
  102.8 0.0 copy-start
  102.8 4.3 %collective-permute-start.4 = (bf16[8,512,128]{2,1,0:T(8,128)(2,1)S(1)}, bf16[8,512,128]{2,1,0:T(8,128)(2,1)S(1)}, u32[]{:S(2)}, u32[]{:S(2)}) collective-permute-start(bf16[8,512,128]{2,1,0:T(8,128)(2,1)S(1)} %all_to_all.21.mine), channel_id=1, source_target_pairs={{0,16},{16,0},{1,17},{17,1},{2,18},{18,2},{3,19},{19,3},{4,20},{20... | collective-permute-start | bytes 3145736 | tf_op jit(solution)/shard_map/ppermute | solution.py:263
  107.1 0.6 pad_add_fusion.place
  107.7 0.0 all-gather.6.cloned.1.call-done
  107.7 1.7 %collective-permute-done.4.theirs = bf16[8,512,128]{2,1,0:T(8,128)(2,1)S(1)} collective-permute-done((bf16[8,512,128]{2,1,0:T(8,128)(2,1)S(1)}, bf16[8,512,128]{2,1,0:T(8,128)(2,1)S(1)}, u32[]{:S(2)}, u32[]{:S(2)}) %collective-permute-start.4) | collective-permute-done | bytes 1048608 | tf_op jit(solution)/shard_map/ppermute | solution.py:263
  109.4 0.0 copy-start.2
  109.4 0.0 copy-done
  109.4 1.0 copy-done.2
  110.4 4.3 %shard_map.78 = bf16[4,2,2,2,64,128]{5,4,3,2,1,0:T(8,128)(2,1)} custom-call(bf16[8,4,64,512]{3,2,1,0:T(8,128)(2,1)} %bitcast.31, bf16[8,512,128]{2,1,0:T(8,128)(2,1)} %copy-done, bf16[8,512,128]{2,1,0:T(8,128)(2,1)} %copy-done.2, s32[2]{0:T(128)} %pad_add_fusion.place), custom_call_target="tpu_custom_call" | custom-call | flops 1073741824 | bytes 5000000 | tf_op jit(solution)/shard_map/pallas_call | solution.py:182
  114.7 23.1 %all_to_all.22 = bf16[32,64,128]{2,1,0:T(8,128)(2,1)S(1)} all-to-all(bf16[32,64,128]{2,1,0:T(8,128)(2,1)} %bitcast.32), channel_id=1, replica_groups=mesh['za'=2,'zb'=4,'xl'=2,'core'=2,'xh'=2,'yh'=4,'yl'=2] {'yh','core','x..., dimensions={0} | all-to-all | bytes 1048576 | tf_op jit(solution)/shard_map/all_to_all | solution.py:267
  137.8 0.7 slice_reduce_fusion
  (2 shorter events, 0.0 us)
Async XLA Ops:
  6.5 27.1 %copy-start.3 = (s32[128]{0:T(128)S(1)}, s32[128]{0:T(128)}, u32[]{:S(2)}) copy-start(s32[128]{0:T(128)} %param.12) | copy-start | bytes 1540
  6.5 47.0 %all-gather.8.cloned.1.call-start = ((), (), s32[]{:S(2)}) async-start(), calls=%async_computation.5 | async-start | bytes 1363968 | tf_op jit(solution)/shard_map/all_gather | solution.py:228
  9.7 27.1 %all-to-all-start = ((bf16[16,96,128]{2,1,0:T(8,128)(2,1)}), bf16[16,96,128]{2,1,0:T(8,128)(2,1)S(1)}, u32[]{:S(2)}, u32[]{:S(2)}) async-start(bf16[16,96,128]{2,1,0:T(8,128)(2,1)} %broadcast_in_dim.12), calls=%async_computation | async-start | bytes 786432 | tf_op jit(solution)/shard_map/all_to_all | solution.py:203
  19.9 87.8 %all-gather.6.cloned.1.call-start = ((), (), s32[]{:S(2)}) async-start(), calls=%async_computation.4 | async-start | bytes 2359296 | tf_op jit(solution)/shard_map/all_gather | solution.py:242
  20.9 19.7 %collective-permute-start = (bf16[56,512]{1,0:T(8,128)(2,1)S(1)}, bf16[56,512]{1,0:T(8,128)(2,1)S(1)}, u32[]{:S(2)}, u32[]{:S(2)}) collective-permute-start(bf16[56,512]{1,0:T(8,128)(2,1)S(1)} %get-tuple-element.22), channel_id=1, source_target_pairs={{0,0},{1,32},{8,8},{9,40},{32,1},{33,33},{40,9},{41,41},{2,2},{3,3... | collective-permute-start | bytes 172040 | tf_op jit(solution)/shard_map/ppermute | solution.py:219
  21.6 19.1 %collective-permute-start.1 = (bf16[56,512]{1,0:T(8,128)(2,1)S(1)}, bf16[56,512]{1,0:T(8,128)(2,1)S(1)}, u32[]{:S(2)}, u32[]{:S(2)}) collective-permute-start(bf16[56,512]{1,0:T(8,128)(2,1)S(1)} %get-tuple-element.21), channel_id=1, source_target_pairs={{0,8},{1,40},{8,0},{9,32},{32,9},{33,41},{40,1},{41,33},{2,10},{3,... | collective-permute-start | bytes 172040 | tf_op jit(solution)/shard_map/ppermute | solution.py:219
  26.4 14.3 %collective-permute-start.2 = (bf16[56,512]{1,0:T(8,128)(2,1)S(1)}, bf16[56,512]{1,0:T(8,128)(2,1)S(1)}, u32[]{:S(2)}, u32[]{:S(2)}) collective-permute-start(bf16[56,512]{1,0:T(8,128)(2,1)S(1)} %get-tuple-element.20), channel_id=1, source_target_pairs={{0,32},{1,0},{8,40},{9,8},{32,33},{33,1},{40,41},{41,9},{2,34},{3,... | collective-permute-start | bytes 172040 | tf_op jit(solution)/shard_map/ppermute | solution.py:219
  31.0 9.6 %collective-permute-start.3 = (bf16[56,512]{1,0:T(8,128)(2,1)S(1)}, bf16[56,512]{1,0:T(8,128)(2,1)S(1)}, u32[]{:S(2)}, u32[]{:S(2)}) collective-permute-start(bf16[56,512]{1,0:T(8,128)(2,1)S(1)} %get-tuple-element.19), channel_id=1, source_target_pairs={{0,40},{1,8},{8,32},{9,0},{32,41},{33,9},{40,33},{41,1},{2,42},{3,... | collective-permute-start | bytes 172040 | tf_op jit(solution)/shard_map/ppermute | solution.py:219
  36.8 0.7 copy-start.1
  102.8 6.5 %copy-start = (bf16[8,512,128]{2,1,0:T(8,128)(2,1)}, bf16[8,512,128]{2,1,0:T(8,128)(2,1)S(1)}, u32[]{:S(2)}) copy-start(bf16[8,512,128]{2,1,0:T(8,128)(2,1)S(1)} %all_to_all.21.mine) | copy-start | bytes 3145732
  102.8 6.5 %collective-permute-start.4 = (bf16[8,512,128]{2,1,0:T(8,128)(2,1)S(1)}, bf16[8,512,128]{2,1,0:T(8,128)(2,1)S(1)}, u32[]{:S(2)}, u32[]{:S(2)}) collective-permute-start(bf16[8,512,128]{2,1,0:T(8,128)(2,1)S(1)} %all_to_all.21.mine), channel_id=1, source_target_pairs={{0,16},{16,0},{1,17},{17,1},{2,18},{18,2},{3,19},{19,3},{4,20},{20... | collective-permute-start | bytes 3145736 | tf_op jit(solution)/shard_map/ppermute | solution.py:263
  109.4 1.0 copy-start.2
Sparse Core Ops, SparseCore 0:
  9.4 43.9 all-gather.7
  55.5 42.6 all-gather.5

commit v5 on v4

--- a/solution.py
+++ b/solution.py
@@ -101,35 +101,33 @@
         key_cat[h, :, :NOPE] = expanded[:, h * NOPE : (h + 1) * NOPE]
         key_cat[h, :, NOPE:] = rope_keys[...]
     positions = key_pos[...]
-    for pair in range(tokens // 2):
-        two = (2 * pair, 2 * pair + 1)
-        q_pos = jnp.concatenate(
-            [queries[t, HEADS * QD : HEADS * QD + 2, :].astype(F32) for t in two], axis=1
-        )
-        q_pos = q_pos[0:1] * 64.0 + q_pos[1:2]
-        visible = positions <= q_pos
-        stats = []
-        for h in range(HEADS):
-            q = jnp.concatenate([queries[t, h * QD : (h + 1) * QD, :] for t in two], axis=1)
-            scores = jnp.where(visible, dot(key_cat[h], q) * scale, masked)
-            largest = jnp.maximum(jnp.max(scores, axis=0, keepdims=True), floor)
-            weights = jnp.exp2(scores - largest)
-            total = jnp.sum(weights, axis=0, keepdims=True)
-            some = total > 0.0
-            safe = jnp.where(some, total, 1.0)
-            summed = dot(value_t[h * VDIM : (h + 1) * VDIM, :], weights.astype(BF16)) / safe
-            level = jnp.where(some, largest + jnp.log2(safe), masked)
-            first = level.astype(BF16)
-            rest = level - first.astype(F32)
-            second = rest.astype(BF16)
-            third = (rest - second.astype(F32)).astype(BF16)
-            stats += [first.astype(F32), second.astype(F32), third.astype(F32)]
-            summed = summed.astype(BF16)
-            for i, t in enumerate(two):
-                out[t, h * VDIM : (h + 1) * VDIM, :] = summed[:, i * TOK : (i + 1) * TOK]
-        stats = jnp.concatenate(stats + [jnp.zeros_like(stats[0])] * 4, axis=0).astype(BF16)
-        for i, t in enumerate(two):
-            out[t, HEADS * VDIM :, :] = stats[:, i * TOK : (i + 1) * TOK]
+    q_pos = jnp.concatenate(
+        [queries[t, HEADS * QD : HEADS * QD + 2, :].astype(F32) for t in range(tokens)], axis=1
+    )
+    q_pos = q_pos[0:1] * 64.0 + q_pos[1:2]
+    stats = []
+    visible = positions <= q_pos
+    for h in range(HEADS):
+        q = jnp.concatenate([queries[t, h * QD : (h + 1) * QD, :] for t in range(tokens)], axis=1)
+        scores = jnp.where(visible, dot(key_cat[h], q) * scale, masked)
+        largest = jnp.maximum(jnp.max(scores, axis=0, keepdims=True), floor)
+        weights = jnp.exp2(scores - largest)
+        total = jnp.sum(weights, axis=0, keepdims=True)
+        some = total > 0.0
+        safe = jnp.where(some, total, 1.0)
+        summed = dot(value_t[h * VDIM : (h + 1) * VDIM, :], weights.astype(BF16)) * (1.0 / safe)
+        level = jnp.where(some, largest + jnp.log2(safe), masked)
+        first = level.astype(BF16)
+        rest = level - first.astype(F32)
+        second = rest.astype(BF16)
+        third = (rest - second.astype(F32)).astype(BF16)
+        stats += [first.astype(F32), second.astype(F32), third.astype(F32)]
+        summed = summed.astype(BF16)
+        for t in range(tokens):
+            out[t, h * VDIM : (h + 1) * VDIM, :] = summed[:, t * TOK : (t + 1) * TOK]
+    stats = jnp.concatenate(stats + [jnp.zeros_like(stats[0])] * 4, axis=0).astype(BF16)
+    for t in range(tokens):
+        out[t, HEADS * VDIM :, :] = stats[:, t * TOK : (t + 1) * TOK]
 
 
 def merge_body(parts, out):

time: 147 us -> 145 us (0.986)
  Pallas kernels: 23.3 us -> 21.4 us
    pallas_call x5, Pallas kernels: 19 us -> 17.1 us  [kernel_call(): pl.pallas_call(body, out_shape=outs[0] if single else outs, in_specs=spec...]
  transfers between devices with their start and end apart: 8 -> 8, of which waited for: 1 -> 1; matrix products, arithmetic and copies ran while one was open for 4% -> 4% of each run, Pallas kernels for 12% -> 11%
where the time goes in v5:
time: 145 us; the launch traced here: 143 us
  blocking collectives  71.5 us (49%)
  starting transfers between devices  26.5 us (18%)
  Pallas kernels  21.4 us (15%)
  between operations  14.2 us (10%)
  local copies, waits for them, and re-layouts  5.25 us (4%)
  other arithmetic  2.8 us (2%)
  waiting for transfers between devices  1.72 us (1%)
    all_to_all x1, blocking collectives, shards(): lax.all_to_all(partial, ('yh', 'core', 'xh', 'xl'), split_axis=0, concat_...  23.1 us
    all_to_all x1, blocking collectives, sent_to_all(): return lax.all_to_all(copies, axis, split_axis=0, concat_axis=0, tiled=True)  19.1 us
    all_to_all x1, blocking collectives, shards(): parts = lax.all_to_all(parts, NEAR, split_axis=0, concat_axis=0, tiled=True)  17.3 us
    pallas_call x5, Pallas kernels, kernel_call(): pl.pallas_call(body, out_shape=outs[0] if single else outs, in_specs=spec...  17.1 us
    all_gather x1, blocking collectives, shards(): queries = lax.all_gather(query, NEAR, axis=0, tiled=False)  12 us
    ppermute x4, starting transfers between devices, shards(): lax.ppermute(lax.dynamic_index_in_dim(columns, (xh ^ half) * 2 + (yl ^ fl...  12 us
    all_to_all x1, starting transfers between devices, sent_to_all(): return lax.all_to_all(copies, axis, split_axis=0, concat_axis=0, tiled=True)  10.2 us
    pallas_call x1, Pallas kernels, project(): pl.pallas_call(project_body, grid=(groups // 2,), out_shape=jax.ShapeDtyp...  4.32 us
  transfers between devices with their start and end apart: 8, of which 1 were waited for; matrix products, arithmetic and copies ran while one was open for 4% of the time, Pallas kernels for 11%

profile of v5, /device:TPU:1, one launch (start us, length us, event | category | flops | bytes accessed | tf_op | source)
XLA Modules:
  0.0 143.3 jit_solution(12779060667833845769)
XLA Ops:
  6.5 0.0 copy-start.3
  6.5 0.0 all-gather.8.cloned.1.call-start
  6.5 1.6 %shard_map.74 = bf16[592,128]{1,0:T(8,128)(2,1)} custom-call(bf16[576,128]{1,0:T(8,128)(2,1)} %bitcast.37, s32[1,128]{1,0:T(1,128)} %bitcast.43), custom_call_target="tpu_custom_call" | custom-call | bytes 4000000 | tf_op jit(solution)/shard_map/pallas_call | solution.py:44
  8.1 0.0 all-gather.8.cloned.1.call-update
  8.2 1.5 %broadcast_in_dim.12 = bf16[16,96,128]{2,1,0:T(8,128)(2,1)} broadcast(bf16[96,128]{1,0:T(8,128)(2,1)} %bitcast.42), dimensions={1,2} | broadcast | bytes 417792 | tf_op jit(solution)/shard_map/broadcast_in_dim | solution.py:200
  9.7 10.2 %all-to-all-start = ((bf16[16,96,128]{2,1,0:T(8,128)(2,1)}), bf16[16,96,128]{2,1,0:T(8,128)(2,1)S(1)}, u32[]{:S(2)}, u32[]{:S(2)}) async-start(bf16[16,96,128]{2,1,0:T(8,128)(2,1)} %broadcast_in_dim.12), calls=%async_computation | async-start | bytes 786432 | tf_op jit(solution)/shard_map/all_to_all | solution.py:201
  19.9 0.0 all-gather.6.cloned.1.call-start
  20.0 0.9 dynamic-slice_bitcast_fusion
  20.9 0.7 collective-permute-start
  21.6 4.8 %collective-permute-start.1 = (bf16[56,512]{1,0:T(8,128)(2,1)S(1)}, bf16[56,512]{1,0:T(8,128)(2,1)S(1)}, u32[]{:S(2)}, u32[]{:S(2)}) collective-permute-start(bf16[56,512]{1,0:T(8,128)(2,1)S(1)} %get-tuple-element.21), channel_id=1, source_target_pairs={{0,8},{1,40},{8,0},{9,32},{32,9},{33,41},{40,1},{41,33},{2,10},{3,... | collective-permute-start | bytes 172040 | tf_op jit(solution)/shard_map/ppermute | solution.py:217
  26.4 4.6 %collective-permute-start.2 = (bf16[56,512]{1,0:T(8,128)(2,1)S(1)}, bf16[56,512]{1,0:T(8,128)(2,1)S(1)}, u32[]{:S(2)}, u32[]{:S(2)}) collective-permute-start(bf16[56,512]{1,0:T(8,128)(2,1)S(1)} %get-tuple-element.20), channel_id=1, source_target_pairs={{0,32},{1,0},{8,40},{9,8},{32,33},{33,1},{40,41},{41,9},{2,34},{3,... | collective-permute-start | bytes 172040 | tf_op jit(solution)/shard_map/ppermute | solution.py:217
  31.0 1.9 %collective-permute-start.3 = (bf16[56,512]{1,0:T(8,128)(2,1)S(1)}, bf16[56,512]{1,0:T(8,128)(2,1)S(1)}, u32[]{:S(2)}, u32[]{:S(2)}) collective-permute-start(bf16[56,512]{1,0:T(8,128)(2,1)S(1)} %get-tuple-element.19), channel_id=1, source_target_pairs={{0,40},{1,8},{8,32},{9,0},{32,41},{33,9},{40,33},{41,1},{2,42},{3,... | collective-permute-start | bytes 172040 | tf_op jit(solution)/shard_map/ppermute | solution.py:217
  33.6 0.0 copy-done.3
  33.6 0.8 multiply_sine_fusion
  34.4 2.4 %shard_map.75 = (bf16[512,512]{1,0:T(8,128)(2,1)}, bf16[512,512]{1,0:T(8,128)(2,1)}) custom-call(bf16[512,1024]{1,0:T(8,128)(2,1)} %w.1), custom_call_target="tpu_custom_call" | custom-call | bytes 4000000 | tf_op jit(solution)/shard_map/pallas_call | solution.py:44
  36.8 0.0 all-to-all-done
  36.8 0.0 copy-start.1
  36.8 0.7 copy-done.1
  37.6 3.1 %shard_map.73 = bf16[784,128]{1,0:T(8,128)(2,1)} custom-call(bf16[1536,128]{1,0:T(8,128)(2,1)} %bitcast.34, bf16[1536,768]{1,0:T(8,128)(2,1)} %weights.1, f32[32,128]{1,0:T(8,128)} %get-tuple-element.24.cosine, f32[32,128]{1,0:T(8,128)} %get-tuple-element.23.sine, s32[1,128]{1,0:T(1,128)} %bitcast.44), custom_call_target="tpu_custom_call" | custom-call | flops 300000000 | bytes 4000000 | tf_op jit(solution)/shard_map/pallas_call | solution.py:44
  40.7 0.0 collective-permute-done
  40.7 0.0 collective-permute-done.1
  40.7 0.0 collective-permute-done.2
  40.7 0.0 collective-permute-done.3
  40.7 0.7 fusion.6
  41.4 0.0 all-gather.6.cloned.1.call-update
  41.5 12.0 %all-gather.1 = bf16[3136,128]{1,0:T(8,128)(2,1)} all-gather(bf16[784,128]{1,0:T(8,128)(2,1)} %shard_map.73), channel_id=3, replica_groups=mesh['za'=2,'zb'=4,'xl'=2,'core'=2,'xh'=2,'yh'=4,'yl'=2] {'xl','core'}, dimensions={0}, use_global_device_ids=true | all-gather | bytes 1003520 | tf_op jit(solution)/shard_map/all_gather | solution.py:241
  53.5 0.0 all-gather.8.cloned.1.call-done
  53.5 8.1 %shard_map.76 = bf16[4,528,128]{2,1,0:T(8,128)(2,1)} custom-call(bf16[4,784,128]{2,1,0:T(8,128)(2,1)} %bitcast.35, bf16[8,592,128]{2,1,0:T(8,128)(2,1)} %bitcast.45, bf16[512,512]{1,0:T(8,128)(2,1)} %get-tuple-element.17.w_key, bf16[512,512]{1,0:T(8,128)(2,1)} %get-tuple-element.18.w_value_t), custom_call_target="tpu_custom_call" | custom-call | flops 3500000000 | bytes 4000000 | tf_op jit(solution)/shard_map/pallas_call | solution.py:44
  61.6 17.3 %all_to_all.20.parts = bf16[4,528,128]{2,1,0:T(8,128)(2,1)} all-to-all(bf16[4,528,128]{2,1,0:T(8,128)(2,1)} %shard_map.76), channel_id=1, replica_groups=mesh['za'=2,'zb'=4,'xl'=2,'core'=2,'xh'=2,'yh'=4,'yl'=2] {'xl','core'}, dimensions={0} | all-to-all | bytes 1081344 | tf_op jit(solution)/shard_map/all_to_all | solution.py:258
  78.9 1.8 %shard_map.77 = bf16[512,128]{1,0:T(8,128)(2,1)} custom-call(bf16[4,528,128]{2,1,0:T(8,128)(2,1)} %all_to_all.20.parts), custom_call_target="tpu_custom_call" | custom-call | flops 1000000 | bytes 4000000 | tf_op jit(solution)/shard_map/pallas_call | solution.py:44
  80.7 1.0 broadcast_in_dim.14
  81.8 19.1 %all_to_all.21.mine = bf16[8,512,128]{2,1,0:T(8,128)(2,1)S(1)} all-to-all(bf16[8,512,128]{2,1,0:T(8,128)(2,1)S(1)} %broadcast_in_dim.14), channel_id=1, replica_groups=mesh['za'=2,'zb'=4,'xl'=2,'core'=2,'xh'=2,'yh'=4,'yl'=2] {'yl','xh','xl'}, dimensions={0} | all-to-all | bytes 2097152 | tf_op jit(solution)/shard_map/all_to_all | solution.py:201
  100.9 0.0 copy-start
  100.9 4.3 %collective-permute-start.4 = (bf16[8,512,128]{2,1,0:T(8,128)(2,1)S(1)}, bf16[8,512,128]{2,1,0:T(8,128)(2,1)S(1)}, u32[]{:S(2)}, u32[]{:S(2)}) collective-permute-start(bf16[8,512,128]{2,1,0:T(8,128)(2,1)S(1)} %all_to_all.21.mine), channel_id=1, source_target_pairs={{0,16},{16,0},{1,17},{17,1},{2,18},{18,2},{3,19},{19,3},{4,20},{20... | collective-permute-start | bytes 3145736 | tf_op jit(solution)/shard_map/ppermute | solution.py:261
  105.1 0.6 pad_add_fusion.place
  105.7 0.0 all-gather.6.cloned.1.call-done
  105.7 1.7 %collective-permute-done.4.theirs = bf16[8,512,128]{2,1,0:T(8,128)(2,1)S(1)} collective-permute-done((bf16[8,512,128]{2,1,0:T(8,128)(2,1)S(1)}, bf16[8,512,128]{2,1,0:T(8,128)(2,1)S(1)}, u32[]{:S(2)}, u32[]{:S(2)}) %collective-permute-start.4) | collective-permute-done | bytes 1048608 | tf_op jit(solution)/shard_map/ppermute | solution.py:261
  107.4 0.0 copy-start.2
  107.4 0.0 copy-done
  107.4 1.0 copy-done.2
  108.4 4.3 %shard_map.78 = bf16[4,2,2,2,64,128]{5,4,3,2,1,0:T(8,128)(2,1)} custom-call(bf16[8,4,64,512]{3,2,1,0:T(8,128)(2,1)} %bitcast.31, bf16[8,512,128]{2,1,0:T(8,128)(2,1)} %copy-done, bf16[8,512,128]{2,1,0:T(8,128)(2,1)} %copy-done.2, s32[2]{0:T(128)} %pad_add_fusion.place), custom_call_target="tpu_custom_call" | custom-call | flops 1073741824 | bytes 5000000 | tf_op jit(solution)/shard_map/pallas_call | solution.py:180
  112.7 23.1 %all_to_all.22 = bf16[32,64,128]{2,1,0:T(8,128)(2,1)S(1)} all-to-all(bf16[32,64,128]{2,1,0:T(8,128)(2,1)} %bitcast.32), channel_id=1, replica_groups=mesh['za'=2,'zb'=4,'xl'=2,'core'=2,'xh'=2,'yh'=4,'yl'=2] {'yh','core','x..., dimensions={0} | all-to-all | bytes 1048576 | tf_op jit(solution)/shard_map/all_to_all | solution.py:265
  135.8 0.7 slice_reduce_fusion
  (2 shorter events, 0.0 us)
Async XLA Ops:
  6.5 27.1 %copy-start.3 = (s32[128]{0:T(128)S(1)}, s32[128]{0:T(128)}, u32[]{:S(2)}) copy-start(s32[128]{0:T(128)} %param.12) | copy-start | bytes 1540
  6.5 47.0 %all-gather.8.cloned.1.call-start = ((), (), s32[]{:S(2)}) async-start(), calls=%async_computation.5 | async-start | bytes 1363968 | tf_op jit(solution)/shard_map/all_gather | solution.py:226
  9.7 27.1 %all-to-all-start = ((bf16[16,96,128]{2,1,0:T(8,128)(2,1)}), bf16[16,96,128]{2,1,0:T(8,128)(2,1)S(1)}, u32[]{:S(2)}, u32[]{:S(2)}) async-start(bf16[16,96,128]{2,1,0:T(8,128)(2,1)} %broadcast_in_dim.12), calls=%async_computation | async-start | bytes 786432 | tf_op jit(solution)/shard_map/all_to_all | solution.py:201
  19.9 85.8 %all-gather.6.cloned.1.call-start = ((), (), s32[]{:S(2)}) async-start(), calls=%async_computation.4 | async-start | bytes 2359296 | tf_op jit(solution)/shard_map/all_gather | solution.py:240
  20.9 19.7 %collective-permute-start = (bf16[56,512]{1,0:T(8,128)(2,1)S(1)}, bf16[56,512]{1,0:T(8,128)(2,1)S(1)}, u32[]{:S(2)}, u32[]{:S(2)}) collective-permute-start(bf16[56,512]{1,0:T(8,128)(2,1)S(1)} %get-tuple-element.22), channel_id=1, source_target_pairs={{0,0},{1,32},{8,8},{9,40},{32,1},{33,33},{40,9},{41,41},{2,2},{3,3... | collective-permute-start | bytes 172040 | tf_op jit(solution)/shard_map/ppermute | solution.py:217
  21.6 19.1 %collective-permute-start.1 = (bf16[56,512]{1,0:T(8,128)(2,1)S(1)}, bf16[56,512]{1,0:T(8,128)(2,1)S(1)}, u32[]{:S(2)}, u32[]{:S(2)}) collective-permute-start(bf16[56,512]{1,0:T(8,128)(2,1)S(1)} %get-tuple-element.21), channel_id=1, source_target_pairs={{0,8},{1,40},{8,0},{9,32},{32,9},{33,41},{40,1},{41,33},{2,10},{3,... | collective-permute-start | bytes 172040 | tf_op jit(solution)/shard_map/ppermute | solution.py:217
  26.4 14.3 %collective-permute-start.2 = (bf16[56,512]{1,0:T(8,128)(2,1)S(1)}, bf16[56,512]{1,0:T(8,128)(2,1)S(1)}, u32[]{:S(2)}, u32[]{:S(2)}) collective-permute-start(bf16[56,512]{1,0:T(8,128)(2,1)S(1)} %get-tuple-element.20), channel_id=1, source_target_pairs={{0,32},{1,0},{8,40},{9,8},{32,33},{33,1},{40,41},{41,9},{2,34},{3,... | collective-permute-start | bytes 172040 | tf_op jit(solution)/shard_map/ppermute | solution.py:217
  31.0 9.6 %collective-permute-start.3 = (bf16[56,512]{1,0:T(8,128)(2,1)S(1)}, bf16[56,512]{1,0:T(8,128)(2,1)S(1)}, u32[]{:S(2)}, u32[]{:S(2)}) collective-permute-start(bf16[56,512]{1,0:T(8,128)(2,1)S(1)} %get-tuple-element.19), channel_id=1, source_target_pairs={{0,40},{1,8},{8,32},{9,0},{32,41},{33,9},{40,33},{41,1},{2,42},{3,... | collective-permute-start | bytes 172040 | tf_op jit(solution)/shard_map/ppermute | solution.py:217
  36.8 0.7 copy-start.1
  100.9 6.5 %copy-start = (bf16[8,512,128]{2,1,0:T(8,128)(2,1)}, bf16[8,512,128]{2,1,0:T(8,128)(2,1)S(1)}, u32[]{:S(2)}) copy-start(bf16[8,512,128]{2,1,0:T(8,128)(2,1)S(1)} %all_to_all.21.mine) | copy-start | bytes 3145732
  100.9 6.5 %collective-permute-start.4 = (bf16[8,512,128]{2,1,0:T(8,128)(2,1)S(1)}, bf16[8,512,128]{2,1,0:T(8,128)(2,1)S(1)}, u32[]{:S(2)}, u32[]{:S(2)}) collective-permute-start(bf16[8,512,128]{2,1,0:T(8,128)(2,1)S(1)} %all_to_all.21.mine), channel_id=1, source_target_pairs={{0,16},{16,0},{1,17},{17,1},{2,18},{18,2},{3,19},{19,3},{4,20},{20... | collective-permute-start | bytes 3145736 | tf_op jit(solution)/shard_map/ppermute | solution.py:261
  107.4 1.0 copy-start.2
Sparse Core Ops, SparseCore 0:
  9.4 43.9 all-gather.7
  55.5 42.6 all-gather.5
